TPU v7x, 32 devices: a whole 2x2x4 slice. The times are simulated.
32 devices in a mesh: bx: 4 (over y, x), by: 2 (over core), bz: 4 (over z).
Axes of the slice: x: 2, y: 2, z: 4, core: 2. Of those that a mesh axis runs over, the one named last changes fastest.
Arguments:
- counts: bfloat16 [64, 64, 128, 128], P(('bx', 'by', 'bz')), may hold values from 0.099609375 to 10
- row_split: bfloat16 [64, 64, 128, 256], P(('bx', 'by', 'bz')), may hold values from 0 to 0.03125
- col_split: bfloat16 [64, 64, 128, 256], P(('bx', 'by', 'bz')), may hold values from 0 to 0.03125
- efficiency: bfloat16 [64, 128, 128], replicated, may hold values from 0.5 to 1.5
- lorentz: float32 [3600], replicated, may hold values from 0.3 to 3
- angles: int32 [64], P(('bx', 'by', 'bz')), may hold values from 0 to 3599
- tile_owner: int32 [4096, 1], P(('bx', 'by', 'bz')), may hold values from 0 to 31; in each aligned block of 128 rows (0 to 127, 128 to 255, ...) at most 16 rows name the same one
- tile_box: int32 [4096], P(('bx', 'by', 'bz')), may hold values from 0 to 511
Outputs:
- intensity: float32 [8, 8, 4, 64, 256], P('bx', 'by', 'bz')
Inputs may be any that keep to these rules, and one draw needn't show every extreme that they name: `tile_owner`: among the 128 tiles of one device, no owner is named more than 16 times, a bound that some block reaches.
All inputs are finite; a program needn't handle non-finite values.
Results may differ from a plain program's by a relative error of at most 0.0003.
Values sent between devices are 32-bit elements; how exact they have to be, the bound alone decides.
No kernel may reach another device: no remote copies, remote signals or barrier semaphores. Data moves between devices by JAX's collectives and lax.ppermute only.
A program may use at most 128 MiB of HBM per device.

v0:
```python
import functools

import jax
import jax.numpy as jnp
from jax import lax
from jax.experimental import pallas as pl
from jax.experimental.pallas import tpu as pltpu
from jax.sharding import PartitionSpec as P

VOX = 256
LANES = 128
GX = 8
GY = 8
GZ = 4
BOX_BRICK = 64
FLIP_VOX = (0b11100000, 0b00011100, 0b00000011)
FLIP_BOX = (0b110000, 0b001100, 0b000011)
AXES = ("bx", "by", "bz")
POSITIONS = 8
TILE_LIMIT = 56 * 1024 * 1024
VMEM_LIMIT = 24 * 1024 * 1024
LARGE = 10**10


class Plan:
    def __init__(self, mesh):
        self.sx, self.sy, self.sz = (mesh.shape[name] for name in AXES)
        self.devices = self.sx * self.sy * self.sz
        lx, ly, lz = GX // self.sx, GY // self.sy, GZ // self.sz
        self.boxes = lx * ly * lz * BOX_BRICK
        self.share = self.boxes // 8
        self.flip_dev = ((self.sx - 1) * self.sy * self.sz, (self.sy - 1) * self.sz, self.sz - 1)
        self.half = (self.sx * self.sy * self.sz // 2, self.sy * self.sz // 2, self.sz // 2)
        self.flip_local = (
            (lx - 1) * ly * lz * BOX_BRICK + FLIP_BOX[0],
            (ly - 1) * lz * BOX_BRICK + FLIP_BOX[1],
            (lz - 1) * BOX_BRICK + FLIP_BOX[2],
        )

    def upper(self, device):
        return [(device & half) != 0 for half in self.half]

    def here(self):
        return (lax.axis_index("bx") * self.sy + lax.axis_index("by")) * self.sz + lax.axis_index("bz")


def masked(flags, masks):
    total = jnp.where(flags[0], masks[0], 0)
    for flag, mask in zip(flags[1:], masks[1:]):
        total = total ^ jnp.where(flag, mask, 0)
    return total


def lane_gather(values, index):
    return jnp.take_along_axis(values, index, axis=1, mode="promise_in_bounds")


def destination(plan, owner, box):
    upper = plan.upper(owner)
    local = box ^ masked(upper, plan.flip_local)
    part = local // plan.share
    row = local % plan.share
    holder = owner ^ masked(upper, plan.flip_dev)
    holder = holder ^ masked([(part & bit) != 0 for bit in (4, 2, 1)], plan.flip_dev)
    return holder * plan.share + row


def accumulate_kernel(plan, angles, lorentz, owner, box, counts, rows, cols, seen, value_out, weight_out, *scratch):
    arrays, sems, turned = scratch[:4], scratch[4], scratch[5]
    frames, positions = counts.shape[0], counts.shape[1]
    blocks = positions // POSITIONS

    def copies(block):
        span = pl.ds(block * POSITIONS, POSITIONS)
        views = [(ref.at[:, span], held.at[:, span]) for ref, held in zip((counts, rows, cols), arrays)]
        views.append((seen.at[span], arrays[3].at[span]))
        return [pltpu.make_async_copy(src, dst, sems.at[block, i]) for i, (src, dst) in enumerate(views)]

    for block in range(blocks):
        for copy in copies(block):
            copy.start()

    tiles = frames * positions
    across = lax.broadcasted_iota(jnp.int32, (tiles, tiles), 1)
    down = lax.broadcasted_iota(jnp.int32, (tiles, tiles), 0)
    flips = masked(plan.upper(owner[...]), FLIP_VOX)
    turned[...] = jnp.sum(jnp.where(across == down, flips, 0), axis=1, keepdims=True)
    ids = destination(plan, owner[...], box[...])
    for out in (value_out, weight_out):
        out[tiles : tiles + 8, :] = jnp.zeros((8, VOX), jnp.float32)
        out[tiles : tiles + 8, :tiles] = jnp.broadcast_to(ids.astype(jnp.float32), (8, tiles))

    @pl.loop(0, blocks)
    def _(block):
        for copy in copies(block):
            copy.wait()
        held_counts, held_rows, held_cols, held_seen = arrays
        lanes = lax.broadcasted_iota(jnp.int32, (POSITIONS, LANES), 1)
        value_rows = [[] for _ in range(frames)]
        weight_rows = [[] for _ in range(frames)]
        for p in range(POSITIONS):
            at = block * POSITIONS + p
            cols_all = jnp.concatenate([held_cols[f, at] for f in range(frames)], axis=1)
            seen_all = jnp.dot(held_seen[at], cols_all, preferred_element_type=jnp.float32)
            for f in range(frames):
                spread = held_rows[f, at].astype(jnp.float32)
                counted = jnp.dot(held_counts[f, at], held_cols[f, at], preferred_element_type=jnp.float32)
                value_rows[f].append(jnp.sum(spread * counted, axis=0, keepdims=True))
                observed = seen_all[:, f * VOX : (f + 1) * VOX]
                weight_rows[f].append(jnp.sum(spread * observed, axis=0, keepdims=True))
        for f in range(frames):
            value = jnp.concatenate(value_rows[f], axis=0) * lorentz[angles[f]]
            weight = jnp.concatenate(weight_rows[f], axis=0)
            place = pl.ds(pl.multiple_of(f * positions + block * POSITIONS, POSITIONS), POSITIONS)
            mask = jnp.broadcast_to(turned[place, :], (POSITIONS, LANES))
            index = lanes ^ (mask & (LANES - 1))
            swap = (mask & LANES) != 0
            for item, out in ((value, value_out), (weight, weight_out)):
                low, high = item[:, :LANES], item[:, LANES:]
                out[place, :LANES] = lane_gather(jnp.where(swap, high, low), index)
                out[place, LANES:] = lane_gather(jnp.where(swap, low, high), index)


def accumulate(plan, counts, row_split, col_split, efficiency, lorentz, angles, owner, box):
    frames, positions, pixels, _ = counts.shape
    tiles = frames * positions
    arrays = (counts, row_split, col_split, efficiency)
    return pl.pallas_call(
        functools.partial(accumulate_kernel, plan),
        in_specs=[pl.BlockSpec(memory_space=pltpu.SMEM)] * 2
        + [pl.BlockSpec(memory_space=pltpu.VMEM)] * 2
        + [pl.BlockSpec(memory_space=pl.ANY)] * 4,
        out_specs=[pl.BlockSpec(memory_space=pltpu.VMEM)] * 2,
        out_shape=[jax.ShapeDtypeStruct((tiles + 8, VOX), jnp.float32)] * 2,
        scratch_shapes=[pltpu.VMEM(array.shape, array.dtype) for array in arrays]
        + [pltpu.SemaphoreType.DMA((positions // POSITIONS, 4)), pltpu.VMEM((tiles, 1), jnp.int32)],
        compiler_params=pltpu.CompilerParams(vmem_limit_bytes=TILE_LIMIT),
        cost_estimate=pl.CostEstimate(
            flops=4 * tiles * pixels * pixels * VOX,
            bytes_accessed=sum(array.size * 2 for array in arrays),
            transcendentals=0,
        ),
        name="tile_sums",
    )(angles, lorentz, owner, box, *arrays)


def scatter_kernel(plan, relative, olds, outs, payload, *refs):
    before, after = refs[:olds], refs[len(refs) - outs :]
    tiles = LANES
    half = payload.shape[0] // 2
    offset = plan.here() if relative else plan.here() & ~((plan.sy - 1) * plan.sz)
    ids = [payload[start + tiles : start + tiles + 1, :tiles] for start in (0, half)]
    ids = jnp.concatenate(ids, axis=1).astype(jnp.int32) ^ (offset * plan.share)
    values = jnp.concatenate([payload[:tiles, :], payload[half : half + tiles, :]], axis=0)
    high = values.astype(jnp.bfloat16)
    low = (values - high.astype(jnp.float32)).astype(jnp.bfloat16)
    for number, out in enumerate(after):
        boxes = lax.broadcasted_iota(jnp.int32, (out.shape[0], ids.shape[1]), 0) + number * out.shape[0]
        pick = (boxes == ids).astype(jnp.float32).astype(jnp.bfloat16)
        total = jnp.dot(pick, high, preferred_element_type=jnp.float32)
        total = total + jnp.dot(pick, low, preferred_element_type=jnp.float32)
        out[...] = total + before[number][...] if olds else total


def stage_kernel(first, second, first_out, second_out):
    first_out[...] = first[...]
    second_out[...] = second[...]


def join_kernel(first, second, *rest):
    half, out = first.shape[0], rest[-1]
    out[:half, :] = first[...]
    out[half:, :] = second[...]


def split_kernel(count, *refs):
    inputs, outs = refs[:-count], refs[-count:]
    share = outs[0].shape[0]
    for number, out in enumerate(outs):
        total = None
        for ref in inputs:
            for start in range(number * share, ref.shape[0], count * share):
                rows = ref[start : start + share, :]
                total = rows if total is None else total + rows
        out[...] = total


def total_kernel(*refs):
    inputs, out = refs[:-1], refs[-1]
    total = inputs[0][...]
    for ref in inputs[1:]:
        total = total + ref[...]
    out[...] = total


def intensity_kernel(value, *refs):
    inputs, out = refs[:-1], refs[-1]
    weight = inputs[0][...]
    for ref in inputs[1:]:
        weight = weight + ref[...]
    out[...] = value[...] * 0.125 / jnp.maximum(weight * 0.125, 1.0)


def unfold_kernel(plan, *refs):
    inputs, out = refs[:-1], refs[-1]
    upper = plan.upper(plan.here())
    own = masked(upper, (4, 2, 1))
    local = masked(upper, plan.flip_local)
    mask = masked(upper, FLIP_VOX)
    index = lax.broadcasted_iota(jnp.int32, (8, LANES), 1) ^ (mask & (LANES - 1))
    turn = lax.broadcasted_iota(jnp.int32, (8, LANES), 0) ^ (local & 7)
    swap = (mask & LANES) != 0
    for relative, ref in enumerate(inputs):
        base = (relative ^ own) * plan.share
        for group in range(0, plan.share, 8):
            rows = ref[group : group + 8, :]
            low, high = rows[:, :LANES], rows[:, LANES:]
            target = (base + group) ^ (local & ~7)
            place = pl.ds(pl.multiple_of(target, 8), 8)
            for at, item in enumerate((jnp.where(swap, high, low), jnp.where(swap, low, high))):
                item = jnp.take_along_axis(item, turn, axis=0, mode="promise_in_bounds")
                out[place, at * LANES : (at + 1) * LANES] = lane_gather(item, index)


def small_call(kernel, shapes, name, *arrays, flops=1):
    return pl.pallas_call(
        kernel,
        out_shape=[jax.ShapeDtypeStruct(shape, jnp.float32) for shape in shapes],
        compiler_params=pltpu.CompilerParams(vmem_limit_bytes=VMEM_LIMIT),
        cost_estimate=pl.CostEstimate(flops=flops, bytes_accessed=1, transcendentals=0),
        name=name,
    )(*arrays)


def shards(plan, counts, row_split, col_split, efficiency, lorentz, angles, tile_owner, tile_box):
    def swap(array, even, odd=None):
        odd = even if odd is None else odd
        pairs = [(i, i ^ (odd if i // plan.sz % 2 else even)) for i in range(plan.devices)]
        return lax.ppermute(array, AXES, pairs)

    def join(first, second, *order):
        rows, width = first.shape
        return small_call(join_kernel, [(2 * rows, width)], "join", first, second, *order)[0]

    row = plan.sy * plan.sz
    owner = tile_owner.reshape(1, -1)
    box = tile_box.reshape(1, -1)
    own = accumulate(plan, counts, row_split, col_split, efficiency, lorentz, angles, owner, box)
    arrived = [swap(array, row, 2 * row) for array in own]
    held = small_call(stage_kernel, [array.shape for array in own], "stage", *own, flops=LARGE)
    near = [join(held[0], arrived[0])]
    near.append(join(held[1], arrived[1], near[0]))
    far = [swap(array, 2 * row, row) for array in near]
    def box_sums(payload, relative, olds, *waits, flops=1):
        count = plan.sy if relative else 1
        kernel = functools.partial(scatter_kernel, plan, relative, len(olds), count)
        shapes = [(row * plan.share // count, VOX)] * count
        return small_call(kernel, shapes, "box_sums", payload, *olds, *waits, flops=flops)

    def spread(arrived):
        kernel = functools.partial(split_kernel, plan.sz)
        parts = small_call(kernel, [(plan.share, VOX)] * plan.sz, "core_sums", *arrived)
        return parts, [parts[0]] + [swap(parts[i], i) for i in range(1, plan.sz)]

    sums = [box_sums(near[0], True, []), box_sums(near[1], True, [], flops=LARGE)]
    value = box_sums(far[0], True, sums[0], sums[1][0])
    weight = box_sums(far[1], True, sums[1], value[0])
    value = [value[0]] + [swap(value[i], i * plan.sz) for i in range(1, plan.sy)]
    weight = [weight[0]] + [swap(weight[i], i * plan.sz) for i in range(1, plan.sy)]
    parts, values = spread(value)
    _, weights = spread(weight)
    (value,) = small_call(total_kernel, [(plan.share, VOX)], "value_total", *values, flops=LARGE)
    (own,) = small_call(intensity_kernel, [(plan.share, VOX)], "intensity", value, *weights)
    flip_x, flip_y, flip_z = plan.flip_dev
    near = [own, swap(own, flip_z), swap(own, flip_x), swap(own, flip_x ^ flip_z)]
    far = [swap(array, flip_y) for array in near]
    ordered = [near[0], near[1], far[0], far[1], near[2], near[3], far[2], far[3]]
    (result,) = small_call(functools.partial(unfold_kernel, plan), [(plan.boxes, VOX)], "unfold", *ordered)
    return result.reshape(GX // plan.sx, GY // plan.sy, GZ // plan.sz, BOX_BRICK, VOX)


def solution(mesh):
    return jax.shard_map(
        functools.partial(shards, Plan(mesh)),
        mesh=mesh,
        in_specs=(
            P(AXES, None, None, None),
            P(AXES, None, None, None),
            P(AXES, None, None, None),
            P(),
            P(),
            P(AXES),
            P(AXES, None),
            P(AXES),
        ),
        out_specs=P("bx", "by", "bz", None, None),
        check_vma=False,
    )
```

profile of v0, /device:TPU:0, one launch (start us, length us, event | category | flops | bytes accessed | tf_op | source)
XLA Modules:
  0.0 56.2 jit_solution(5824225445397815887)
XLA Ops:
  0.0 10.2 %tile_sums.1 = (f32[136,256]{1,0:T(8,128)}, f32[136,256]{1,0:T(8,128)}) custom-call(s32[2]{0:T(128)} %angles.1, f32[3600]{0:T(1024)} %lorentz.1, s32[1,128]{1,0:T(1,128)} %bitcast.5, s32[1,128]{1,0:T(1,128)} %bitcast.6, bf16[2,64,128,128]{3,2,1,0:T(8,128)(2,1)} %counts.1, bf16[2,64,128,256]{3,2,1,0:T(8,128)(2,1)} %rows.1, bf16[2,64,128,256]{3,2,1,0:T(8,128)(2,1)} %cols.1, ...), custom_call_target="tpu_custom_call" | custom-call | flops 2147483648 | bytes 23068672 | tf_op jit(solution)/shard_map/tile_sums/pallas_call | solution.py:128
  10.2 3.0 %collective-permute-start = (f32[136,256]{1,0:T(8,128)}, f32[136,256]{1,0:T(8,128)S(1)}, u32[]{:S(2)}, u32[]{:S(2)}) collective-permute-start(f32[136,256]{1,0:T(8,128)} %get-tuple-element.25.first), channel_id=1, source_target_pairs={{0,8},{1,9},{2,10},{3,11},{4,20},{5,21},{6,22},{7,23},{8,0},{9,1},... | collective-permute-start | bytes 417800 | tf_op jit(solution)/shard_map/ppermute | solution.py:239
  13.3 0.9 %copy-done = f32[136,256]{1,0:T(8,128)S(1)} copy-done((f32[136,256]{1,0:T(8,128)S(1)}, f32[136,256]{1,0:T(8,128)}, u32[]{:S(2)}) %copy-start) | copy-done | bytes 139288
  14.2 0.9 %copy-done.1 = f32[136,256]{1,0:T(8,128)S(1)} copy-done((f32[136,256]{1,0:T(8,128)S(1)}, f32[136,256]{1,0:T(8,128)}, u32[]{:S(2)}) %copy-start.1) | copy-done | bytes 139288
  15.2 1.3 %collective-permute-done.second = f32[136,256]{1,0:T(8,128)S(1)} collective-permute-done((f32[136,256]{1,0:T(8,128)}, f32[136,256]{1,0:T(8,128)S(1)}, u32[]{:S(2)}, u32[]{:S(2)}) %collective-permute-start) | collective-permute-done | bytes 139296 | tf_op jit(solution)/shard_map/ppermute | solution.py:239
  16.5 2.1 %collective-permute-start.1 = (f32[272,256]{1,0:T(8,128)S(1)}, f32[272,256]{1,0:T(8,128)S(1)}, u32[]{:S(2)}, u32[]{:S(2)}) collective-permute-start(f32[272,256]{1,0:T(8,128)S(1)} %join.2.payload.rest_0_), channel_id=1, source_target_pairs={{0,16},{1,17},{2,18},{3,19},{4,12},{5,13},{6,14},{7,15},{8,24},{9,... | collective-permute-start | bytes 835592 | tf_op jit(solution)/shard_map/ppermute | solution.py:239
  18.6 1.5 %collective-permute-start.7 = (f32[272,256]{1,0:T(8,128)S(1)}, f32[272,256]{1,0:T(8,128)S(1)}, u32[]{:S(2)}, u32[]{:S(2)}) collective-permute-start(f32[272,256]{1,0:T(8,128)S(1)} %join.3.payload), channel_id=1, source_target_pairs={{0,16},{1,17},{2,18},{3,19},{4,12},{5,13},{6,14},{7,15},{8,24},{9,... | collective-permute-start | bytes 835592 | tf_op jit(solution)/shard_map/ppermute | solution.py:239
  20.7 2.4 %collective-permute-done.1.payload = f32[272,256]{1,0:T(8,128)S(1)} collective-permute-done((f32[272,256]{1,0:T(8,128)S(1)}, f32[272,256]{1,0:T(8,128)S(1)}, u32[]{:S(2)}, u32[]{:S(2)}) %collective-permute-start.1) | collective-permute-done | bytes 278560 | tf_op jit(solution)/shard_map/ppermute | solution.py:239
  23.5 2.6 %collective-permute-done.7.payload = f32[272,256]{1,0:T(8,128)S(1)} collective-permute-done((f32[272,256]{1,0:T(8,128)S(1)}, f32[272,256]{1,0:T(8,128)S(1)}, u32[]{:S(2)}, u32[]{:S(2)}) %collective-permute-start.7) | collective-permute-done | bytes 278560 | tf_op jit(solution)/shard_map/ppermute | solution.py:239
  26.6 2.1 %collective-permute-start.4 = (f32[64,256]{1,0:T(8,128)S(1)}, f32[64,256]{1,0:T(8,128)S(1)}, u32[]{:S(2)}, u32[]{:S(2)}) collective-permute-start(f32[64,256]{1,0:T(8,128)S(1)} %get-tuple-element.35), channel_id=1, source_target_pairs={{0,1},{1,0},{2,3},{3,2},{4,5},{5,4},{6,7},{7,6},{8,9},{9,8},{10,11... | collective-permute-start | bytes 196616 | tf_op jit(solution)/shard_map/ppermute | solution.py:239
  28.7 2.6 %collective-permute-start.5 = (f32[64,256]{1,0:T(8,128)S(1)}, f32[64,256]{1,0:T(8,128)S(1)}, u32[]{:S(2)}, u32[]{:S(2)}) collective-permute-start(f32[64,256]{1,0:T(8,128)S(1)} %get-tuple-element.36), channel_id=1, source_target_pairs={{0,2},{1,3},{2,0},{3,1},{4,6},{5,7},{6,4},{7,5},{8,10},{9,11},{10,... | collective-permute-start | bytes 196616 | tf_op jit(solution)/shard_map/ppermute | solution.py:239
  31.3 1.0 %collective-permute-start.9 = (f32[64,256]{1,0:T(8,128)S(1)}, f32[64,256]{1,0:T(8,128)S(1)}, u32[]{:S(2)}, u32[]{:S(2)}) collective-permute-start(f32[64,256]{1,0:T(8,128)S(1)} %get-tuple-element.42), channel_id=1, source_target_pairs={{0,1},{1,0},{2,3},{3,2},{4,5},{5,4},{6,7},{7,6},{8,9},{9,8},{10,11... | collective-permute-start | bytes 196616 | tf_op jit(solution)/shard_map/ppermute | solution.py:239
  32.3 3.5 %collective-permute-start.10 = (f32[64,256]{1,0:T(8,128)S(1)}, f32[64,256]{1,0:T(8,128)S(1)}, u32[]{:S(2)}, u32[]{:S(2)}) collective-permute-start(f32[64,256]{1,0:T(8,128)S(1)} %get-tuple-element.43), channel_id=1, source_target_pairs={{0,2},{1,3},{2,0},{3,1},{4,6},{5,7},{6,4},{7,5},{8,10},{9,11},{10,... | collective-permute-start | bytes 196616 | tf_op jit(solution)/shard_map/ppermute | solution.py:239
  35.8 0.3 collective-permute-start.11
  36.1 2.0 %collective-permute-done.6.refs_3_ = f32[64,256]{1,0:T(8,128)S(1)} collective-permute-done((f32[64,256]{1,0:T(8,128)S(1)}, f32[64,256]{1,0:T(8,128)S(1)}, u32[]{:S(2)}, u32[]{:S(2)}) %collective-permute-start.6) | collective-permute-done | bytes 65568 | tf_op jit(solution)/shard_map/ppermute | solution.py:239
  38.1 4.6 %collective-permute-done.10.refs_2_ = f32[64,256]{1,0:T(8,128)S(1)} collective-permute-done((f32[64,256]{1,0:T(8,128)S(1)}, f32[64,256]{1,0:T(8,128)S(1)}, u32[]{:S(2)}, u32[]{:S(2)}) %collective-permute-start.10) | collective-permute-done | bytes 65568 | tf_op jit(solution)/shard_map/ppermute | solution.py:239
  42.7 4.7 %collective-permute-start.16 = (f32[64,256]{1,0:T(8,128)S(1)}, f32[64,256]{1,0:T(8,128)S(1)}, u32[]{:S(2)}, u32[]{:S(2)}) collective-permute-start(f32[64,256]{1,0:T(8,128)S(1)} %intensity.1.refs_0_), channel_id=1, source_target_pairs={{0,27},{1,26},{2,25},{3,24},{4,31},{5,30},{6,29},{7,28},{8,19},{9,... | collective-permute-start | bytes 196616 | tf_op jit(solution)/shard_map/ppermute | solution.py:239
  47.4 0.5 collective-permute-start.15
  47.9 1.1 %collective-permute-start.12 = (f32[64,256]{1,0:T(8,128)S(1)}, f32[64,256]{1,0:T(8,128)S(1)}, u32[]{:S(2)}, u32[]{:S(2)}) collective-permute-start(f32[64,256]{1,0:T(8,128)S(1)} %intensity.1.refs_0_), channel_id=1, source_target_pairs={{0,3},{1,2},{2,1},{3,0},{4,7},{5,6},{6,5},{7,4},{8,11},{9,10},{10,... | collective-permute-start | bytes 196616 | tf_op jit(solution)/shard_map/ppermute | solution.py:239
  49.0 1.7 %collective-permute-done.16.refs_5_ = f32[64,256]{1,0:T(8,128)S(1)} collective-permute-done((f32[64,256]{1,0:T(8,128)S(1)}, f32[64,256]{1,0:T(8,128)S(1)}, u32[]{:S(2)}, u32[]{:S(2)}) %collective-permute-start.16) | collective-permute-done | bytes 65568 | tf_op jit(solution)/shard_map/ppermute | solution.py:239
  50.7 1.9 %collective-permute-done.15.refs_4_ = f32[64,256]{1,0:T(8,128)S(1)} collective-permute-done((f32[64,256]{1,0:T(8,128)S(1)}, f32[64,256]{1,0:T(8,128)S(1)}, u32[]{:S(2)}, u32[]{:S(2)}) %collective-permute-start.15) | collective-permute-done | bytes 65568 | tf_op jit(solution)/shard_map/ppermute | solution.py:239
  52.6 1.4 %collective-permute-done.12.refs_1_ = f32[64,256]{1,0:T(8,128)S(1)} collective-permute-done((f32[64,256]{1,0:T(8,128)S(1)}, f32[64,256]{1,0:T(8,128)S(1)}, u32[]{:S(2)}, u32[]{:S(2)}) %collective-permute-start.12) | collective-permute-done | bytes 65568 | tf_op jit(solution)/shard_map/ppermute | solution.py:239
  54.0 1.2 %collective-permute-done.14.refs_3_ = f32[64,256]{1,0:T(8,128)S(1)} collective-permute-done((f32[64,256]{1,0:T(8,128)S(1)}, f32[64,256]{1,0:T(8,128)S(1)}, u32[]{:S(2)}, u32[]{:S(2)}) %collective-permute-start.14) | collective-permute-done | bytes 65568 | tf_op jit(solution)/shard_map/ppermute | solution.py:239
  55.2 1.0 %unfold.1 = f32[512,256]{1,0:T(8,128)} custom-call(f32[64,256]{1,0:T(8,128)S(1)} %intensity.1.refs_0_, f32[64,256]{1,0:T(8,128)S(1)} %collective-permute-done.12.refs_1_, f32[64,256]{1,0:T(8,128)S(1)} %collective-permute-done.13.refs_2_, f32[64,256]{1,0:T(8,128)S(1)} %collective-permute-done.14.refs_3_, f32[64,256]{1,0:T(8,128)S(1)} %collective-permute-done.15.refs_4_, ...), custom_call_target="tpu_custom_call" | custom-call | flops 1 | bytes 1 | tf_op jit(solution)/shard_map/unfold/pallas_call | solution.py:226
  (31 shorter events, 1.6 us)
Async XLA Ops:
  10.2 6.2 %collective-permute-start = (f32[136,256]{1,0:T(8,128)}, f32[136,256]{1,0:T(8,128)S(1)}, u32[]{:S(2)}, u32[]{:S(2)}) collective-permute-start(f32[136,256]{1,0:T(8,128)} %get-tuple-element.25.first), channel_id=1, source_target_pairs={{0,8},{1,9},{2,10},{3,11},{4,20},{5,21},{6,22},{7,23},{8,0},{9,1},... | collective-permute-start | bytes 417800 | tf_op jit(solution)/shard_map/ppermute | solution.py:239
  13.2 5.4 %collective-permute-start.2 = (f32[136,256]{1,0:T(8,128)}, f32[136,256]{1,0:T(8,128)S(1)}, u32[]{:S(2)}, u32[]{:S(2)}) collective-permute-start(f32[136,256]{1,0:T(8,128)} %get-tuple-element.26.second), channel_id=1, source_target_pairs={{0,8},{1,9},{2,10},{3,11},{4,20},{5,21},{6,22},{7,23},{8,0},{9,1},... | collective-permute-start | bytes 417800 | tf_op jit(solution)/shard_map/ppermute | solution.py:239
  13.3 0.9 %copy-start = (f32[136,256]{1,0:T(8,128)S(1)}, f32[136,256]{1,0:T(8,128)}, u32[]{:S(2)}) copy-start(f32[136,256]{1,0:T(8,128)} %get-tuple-element.26.second) | copy-start | bytes 417796
  14.2 0.9 %copy-start.1 = (f32[136,256]{1,0:T(8,128)S(1)}, f32[136,256]{1,0:T(8,128)}, u32[]{:S(2)}) copy-start(f32[136,256]{1,0:T(8,128)} %get-tuple-element.25.first) | copy-start | bytes 417796
  16.5 6.6 %collective-permute-start.1 = (f32[272,256]{1,0:T(8,128)S(1)}, f32[272,256]{1,0:T(8,128)S(1)}, u32[]{:S(2)}, u32[]{:S(2)}) collective-permute-start(f32[272,256]{1,0:T(8,128)S(1)} %join.2.payload.rest_0_), channel_id=1, source_target_pairs={{0,16},{1,17},{2,18},{3,19},{4,12},{5,13},{6,14},{7,15},{8,24},{9,... | collective-permute-start | bytes 835592 | tf_op jit(solution)/shard_map/ppermute | solution.py:239
  18.6 7.5 %collective-permute-start.7 = (f32[272,256]{1,0:T(8,128)S(1)}, f32[272,256]{1,0:T(8,128)S(1)}, u32[]{:S(2)}, u32[]{:S(2)}) collective-permute-start(f32[272,256]{1,0:T(8,128)S(1)} %join.3.payload), channel_id=1, source_target_pairs={{0,16},{1,17},{2,18},{3,19},{4,12},{5,13},{6,14},{7,15},{8,24},{9,... | collective-permute-start | bytes 835592 | tf_op jit(solution)/shard_map/ppermute | solution.py:239
  23.4 3.1 %collective-permute-start.3 = (f32[256,256]{1,0:T(8,128)S(1)}, f32[256,256]{1,0:T(8,128)S(1)}, u32[]{:S(2)}, u32[]{:S(2)}) collective-permute-start(f32[256,256]{1,0:T(8,128)S(1)} %get-tuple-element.33), channel_id=1, source_target_pairs={{0,4},{1,5},{2,6},{3,7},{4,0},{5,1},{6,2},{7,3},{8,12},{9,13},{10,... | collective-permute-start | bytes 786440 | tf_op jit(solution)/shard_map/ppermute | solution.py:239
  26.4 4.9 %collective-permute-start.8 = (f32[256,256]{1,0:T(8,128)S(1)}, f32[256,256]{1,0:T(8,128)S(1)}, u32[]{:S(2)}, u32[]{:S(2)}) collective-permute-start(f32[256,256]{1,0:T(8,128)S(1)} %get-tuple-element.40), channel_id=1, source_target_pairs={{0,4},{1,5},{2,6},{3,7},{4,0},{5,1},{6,2},{7,3},{8,12},{9,13},{10,... | collective-permute-start | bytes 786440 | tf_op jit(solution)/shard_map/ppermute | solution.py:239
  26.6 9.2 %collective-permute-start.4 = (f32[64,256]{1,0:T(8,128)S(1)}, f32[64,256]{1,0:T(8,128)S(1)}, u32[]{:S(2)}, u32[]{:S(2)}) collective-permute-start(f32[64,256]{1,0:T(8,128)S(1)} %get-tuple-element.35), channel_id=1, source_target_pairs={{0,1},{1,0},{2,3},{3,2},{4,5},{5,4},{6,7},{7,6},{8,9},{9,8},{10,11... | collective-permute-start | bytes 196616 | tf_op jit(solution)/shard_map/ppermute | solution.py:239
  28.7 7.4 %collective-permute-start.5 = (f32[64,256]{1,0:T(8,128)S(1)}, f32[64,256]{1,0:T(8,128)S(1)}, u32[]{:S(2)}, u32[]{:S(2)}) collective-permute-start(f32[64,256]{1,0:T(8,128)S(1)} %get-tuple-element.36), channel_id=1, source_target_pairs={{0,2},{1,3},{2,0},{3,1},{4,6},{5,7},{6,4},{7,5},{8,10},{9,11},{10,... | collective-permute-start | bytes 196616 | tf_op jit(solution)/shard_map/ppermute | solution.py:239
  31.3 6.8 %collective-permute-start.6 = (f32[64,256]{1,0:T(8,128)S(1)}, f32[64,256]{1,0:T(8,128)S(1)}, u32[]{:S(2)}, u32[]{:S(2)}) collective-permute-start(f32[64,256]{1,0:T(8,128)S(1)} %get-tuple-element.37), channel_id=1, source_target_pairs={{0,3},{1,2},{2,1},{3,0},{4,7},{5,6},{6,5},{7,4},{8,11},{9,10},{10,... | collective-permute-start | bytes 196616 | tf_op jit(solution)/shard_map/ppermute | solution.py:239
  31.3 6.8 %collective-permute-start.9 = (f32[64,256]{1,0:T(8,128)S(1)}, f32[64,256]{1,0:T(8,128)S(1)}, u32[]{:S(2)}, u32[]{:S(2)}) collective-permute-start(f32[64,256]{1,0:T(8,128)S(1)} %get-tuple-element.42), channel_id=1, source_target_pairs={{0,1},{1,0},{2,3},{3,2},{4,5},{5,4},{6,7},{7,6},{8,9},{9,8},{10,11... | collective-permute-start | bytes 196616 | tf_op jit(solution)/shard_map/ppermute | solution.py:239
  32.3 10.4 %collective-permute-start.10 = (f32[64,256]{1,0:T(8,128)S(1)}, f32[64,256]{1,0:T(8,128)S(1)}, u32[]{:S(2)}, u32[]{:S(2)}) collective-permute-start(f32[64,256]{1,0:T(8,128)S(1)} %get-tuple-element.43), channel_id=1, source_target_pairs={{0,2},{1,3},{2,0},{3,1},{4,6},{5,7},{6,4},{7,5},{8,10},{9,11},{10,... | collective-permute-start | bytes 196616 | tf_op jit(solution)/shard_map/ppermute | solution.py:239
  35.8 6.9 %collective-permute-start.11 = (f32[64,256]{1,0:T(8,128)S(1)}, f32[64,256]{1,0:T(8,128)S(1)}, u32[]{:S(2)}, u32[]{:S(2)}) collective-permute-start(f32[64,256]{1,0:T(8,128)S(1)} %get-tuple-element.44), channel_id=1, source_target_pairs={{0,3},{1,2},{2,1},{3,0},{4,7},{5,6},{6,5},{7,4},{8,11},{9,10},{10,... | collective-permute-start | bytes 196616 | tf_op jit(solution)/shard_map/ppermute | solution.py:239
  42.7 7.9 %collective-permute-start.16 = (f32[64,256]{1,0:T(8,128)S(1)}, f32[64,256]{1,0:T(8,128)S(1)}, u32[]{:S(2)}, u32[]{:S(2)}) collective-permute-start(f32[64,256]{1,0:T(8,128)S(1)} %intensity.1.refs_0_), channel_id=1, source_target_pairs={{0,27},{1,26},{2,25},{3,24},{4,31},{5,30},{6,29},{7,28},{8,19},{9,... | collective-permute-start | bytes 196616 | tf_op jit(solution)/shard_map/ppermute | solution.py:239
  47.4 5.2 %collective-permute-start.15 = (f32[64,256]{1,0:T(8,128)S(1)}, f32[64,256]{1,0:T(8,128)S(1)}, u32[]{:S(2)}, u32[]{:S(2)}) collective-permute-start(f32[64,256]{1,0:T(8,128)S(1)} %intensity.1.refs_0_), channel_id=1, source_target_pairs={{0,24},{1,25},{2,26},{3,27},{4,28},{5,29},{6,30},{7,31},{8,16},{9,... | collective-permute-start | bytes 196616 | tf_op jit(solution)/shard_map/ppermute | solution.py:239
  47.9 6.1 %collective-permute-start.12 = (f32[64,256]{1,0:T(8,128)S(1)}, f32[64,256]{1,0:T(8,128)S(1)}, u32[]{:S(2)}, u32[]{:S(2)}) collective-permute-start(f32[64,256]{1,0:T(8,128)S(1)} %intensity.1.refs_0_), channel_id=1, source_target_pairs={{0,3},{1,2},{2,1},{3,0},{4,7},{5,6},{6,5},{7,4},{8,11},{9,10},{10,... | collective-permute-start | bytes 196616 | tf_op jit(solution)/shard_map/ppermute | solution.py:239
  49.0 5.0 %collective-permute-start.13 = (f32[64,256]{1,0:T(8,128)S(1)}, f32[64,256]{1,0:T(8,128)S(1)}, u32[]{:S(2)}, u32[]{:S(2)}) collective-permute-start(f32[64,256]{1,0:T(8,128)S(1)} %intensity.1.refs_0_), channel_id=1, source_target_pairs={{0,4},{1,5},{2,6},{3,7},{4,0},{5,1},{6,2},{7,3},{8,12},{9,13},{10,... | collective-permute-start | bytes 196616 | tf_op jit(solution)/shard_map/ppermute | solution.py:239
  50.7 3.3 %collective-permute-start.18 = (f32[64,256]{1,0:T(8,128)S(1)}, f32[64,256]{1,0:T(8,128)S(1)}, u32[]{:S(2)}, u32[]{:S(2)}) collective-permute-start(f32[64,256]{1,0:T(8,128)S(1)} %collective-permute-done.16.refs_5_), channel_id=1, source_target_pairs={{0,4},{1,5},{2,6},{3,7},{4,0},{5,1},{6,2},{7,3},{8,12},{9,13},{10,... | collective-permute-start | bytes 196616 | tf_op jit(solution)/shard_map/ppermute | solution.py:239
  52.6 1.4 %collective-permute-start.17 = (f32[64,256]{1,0:T(8,128)S(1)}, f32[64,256]{1,0:T(8,128)S(1)}, u32[]{:S(2)}, u32[]{:S(2)}) collective-permute-start(f32[64,256]{1,0:T(8,128)S(1)} %collective-permute-done.15.refs_4_), channel_id=1, source_target_pairs={{0,4},{1,5},{2,6},{3,7},{4,0},{5,1},{6,2},{7,3},{8,12},{9,13},{10,... | collective-permute-start | bytes 196616 | tf_op jit(solution)/shard_map/ppermute | solution.py:239
  53.9 1.3 %collective-permute-start.14 = (f32[64,256]{1,0:T(8,128)S(1)}, f32[64,256]{1,0:T(8,128)S(1)}, u32[]{:S(2)}, u32[]{:S(2)}) collective-permute-start(f32[64,256]{1,0:T(8,128)S(1)} %collective-permute-done.12.refs_1_), channel_id=1, source_target_pairs={{0,4},{1,5},{2,6},{3,7},{4,0},{5,1},{6,2},{7,3},{8,12},{9,13},{10,... | collective-permute-start | bytes 196616 | tf_op jit(solution)/shard_map/ppermute | solution.py:239
where the time goes:
time: 56.4 us; the launch traced here: 56.2 us
  starting transfers between devices  22.6 us (40%)
  waiting for transfers between devices  19.1 us (34%)
  Pallas kernels  12.6 us (22%)
  local copies, waits for them, and re-layouts  1.85 us (3%)
    ppermute x19, starting transfers between devices, swap(): return lax.ppermute(array, AXES, pairs)  22.6 us
    ppermute x19, waiting for transfers between devices, swap(): return lax.ppermute(array, AXES, pairs)  19.1 us
    pallas_call x1, Pallas kernels, accumulate(): pl.pallas_call(functools.partial(accumulate_kernel, plan), in_specs=[pl.B...  10.2 us
    pallas_call x12, Pallas kernels, small_call(): pl.pallas_call(kernel, out_shape=[jax.ShapeDtypeStruct(shape, jnp.float32...  2.37 us
    unnamed x4, local copies, waits for them, and re-layouts  1.85 us
  transfers between devices with their start and end apart: 19, of which 9 were waited for; matrix products, arithmetic and copies ran while one was open for 0% of the time, Pallas kernels for 2%

commit v1 on v0

--- a/solution.py
+++ b/solution.py
@@ -20,6 +20,7 @@
 TILE_LIMIT = 56 * 1024 * 1024
 VMEM_LIMIT = 24 * 1024 * 1024
 LARGE = 10**10
+UNFOLD_ORDER = (7, 5, 6, 4, 3, 1, 2, 0)
 
 
 class Plan:
@@ -40,6 +41,19 @@
     def upper(self, device):
         return [(device & half) != 0 for half in self.half]
 
+    def steps(self):
+        row = self.sy * self.sz
+        return (row, 1), (2 * row, 2)
+
+    def box_row(self, place):
+        (gather_a, gather_b), (first, second) = self.steps()
+        has = lambda mask: (place & (mask * self.share)) != 0
+        other_y = place // (self.sz * self.share) % self.sy
+        odd = ((other_y ^ lax.axis_index("by")) & 1) != 0
+        part = jnp.where(has(first), jnp.where(odd, 1, 2), 0) + jnp.where(has(second), jnp.where(odd, 2, 1), 0)
+        row = (other_y * 4 + part) * self.share + place % self.share
+        return jnp.where(has(gather_a) | has(gather_b), -1, row)
+
     def here(self):
         return (lax.axis_index("bx") * self.sy + lax.axis_index("by")) * self.sz + lax.axis_index("bz")
 
@@ -66,7 +80,7 @@
 
 
 def accumulate_kernel(plan, angles, lorentz, owner, box, counts, rows, cols, seen, value_out, weight_out, *scratch):
-    arrays, sems, turned = scratch[:4], scratch[4], scratch[5]
+    arrays, sems, turned, partial = scratch[:4], scratch[4], scratch[5], scratch[6]
     frames, positions = counts.shape[0], counts.shape[1]
     blocks = positions // POSITIONS
 
@@ -96,8 +110,6 @@
             copy.wait()
         held_counts, held_rows, held_cols, held_seen = arrays
         lanes = lax.broadcasted_iota(jnp.int32, (POSITIONS, LANES), 1)
-        value_rows = [[] for _ in range(frames)]
-        weight_rows = [[] for _ in range(frames)]
         for p in range(POSITIONS):
             at = block * POSITIONS + p
             cols_all = jnp.concatenate([held_cols[f, at] for f in range(frames)], axis=1)
@@ -105,20 +117,24 @@
             for f in range(frames):
                 spread = held_rows[f, at].astype(jnp.float32)
                 counted = jnp.dot(held_counts[f, at], held_cols[f, at], preferred_element_type=jnp.float32)
-                value_rows[f].append(jnp.sum(spread * counted, axis=0, keepdims=True))
                 observed = seen_all[:, f * VOX : (f + 1) * VOX]
-                weight_rows[f].append(jnp.sum(spread * observed, axis=0, keepdims=True))
+                for kind, item in enumerate((counted, observed)):
+                    product = jnp.sum((spread * item).reshape(-1, 8, VOX), axis=0)
+                    partial[f, kind, 0, p * 8 : (p + 1) * 8, :] = product[:, :LANES]
+                    partial[f, kind, 1, p * 8 : (p + 1) * 8, :] = product[:, LANES:]
         for f in range(frames):
-            value = jnp.concatenate(value_rows[f], axis=0) * lorentz[angles[f]]
-            weight = jnp.concatenate(weight_rows[f], axis=0)
             place = pl.ds(pl.multiple_of(f * positions + block * POSITIONS, POSITIONS), POSITIONS)
             mask = jnp.broadcast_to(turned[place, :], (POSITIONS, LANES))
             index = lanes ^ (mask & (LANES - 1))
             swap = (mask & LANES) != 0
-            for item, out in ((value, value_out), (weight, weight_out)):
-                low, high = item[:, :LANES], item[:, LANES:]
-                out[place, :LANES] = lane_gather(jnp.where(swap, high, low), index)
-                out[place, LANES:] = lane_gather(jnp.where(swap, low, high), index)
+            for kind, out in enumerate((value_out, weight_out)):
+                low, high = (
+                    sum(partial[f, kind, half, pl.ds(row, POSITIONS, stride=8), :] for row in range(8))
+                    for half in range(2)
+                )
+                scale = lorentz[angles[f]] if kind == 0 else 1.0
+                out[place, :LANES] = lane_gather(jnp.where(swap, high, low), index) * scale
+                out[place, LANES:] = lane_gather(jnp.where(swap, low, high), index) * scale
 
 
 def accumulate(plan, counts, row_split, col_split, efficiency, lorentz, angles, owner, box):
@@ -133,7 +149,11 @@
         out_specs=[pl.BlockSpec(memory_space=pltpu.VMEM)] * 2,
         out_shape=[jax.ShapeDtypeStruct((tiles + 8, VOX), jnp.float32)] * 2,
         scratch_shapes=[pltpu.VMEM(array.shape, array.dtype) for array in arrays]
-        + [pltpu.SemaphoreType.DMA((positions // POSITIONS, 4)), pltpu.VMEM((tiles, 1), jnp.int32)],
+        + [
+            pltpu.SemaphoreType.DMA((positions // POSITIONS, 4)),
+            pltpu.VMEM((tiles, 1), jnp.int32),
+            pltpu.VMEM((frames, 2, 2, 8 * POSITIONS, LANES), jnp.float32),
+        ],
         compiler_params=pltpu.CompilerParams(vmem_limit_bytes=TILE_LIMIT),
         cost_estimate=pl.CostEstimate(
             flops=4 * tiles * pixels * pixels * VOX,
@@ -144,13 +164,12 @@
     )(angles, lorentz, owner, box, *arrays)
 
 
-def scatter_kernel(plan, relative, olds, outs, payload, *refs):
+def scatter_kernel(plan, olds, outs, payload, *refs):
     before, after = refs[:olds], refs[len(refs) - outs :]
     tiles = LANES
     half = payload.shape[0] // 2
-    offset = plan.here() if relative else plan.here() & ~((plan.sy - 1) * plan.sz)
     ids = [payload[start + tiles : start + tiles + 1, :tiles] for start in (0, half)]
-    ids = jnp.concatenate(ids, axis=1).astype(jnp.int32) ^ (offset * plan.share)
+    ids = plan.box_row(jnp.concatenate(ids, axis=1).astype(jnp.int32) ^ (plan.here() * plan.share))
     values = jnp.concatenate([payload[:tiles, :], payload[half : half + tiles, :]], axis=0)
     high = values.astype(jnp.bfloat16)
     low = (values - high.astype(jnp.float32)).astype(jnp.bfloat16)
@@ -173,24 +192,16 @@
     out[half:, :] = second[...]
 
 
-def split_kernel(count, *refs):
-    inputs, outs = refs[:-count], refs[-count:]
-    share = outs[0].shape[0]
-    for number, out in enumerate(outs):
-        total = None
-        for ref in inputs:
-            for start in range(number * share, ref.shape[0], count * share):
-                rows = ref[start : start + share, :]
-                total = rows if total is None else total + rows
+def add_kernel(count, *refs):
+    inputs, outs = refs[:count], refs[count:]
+    start = 0
+    for out in outs:
+        span = slice(start, start + out.shape[0])
+        total = inputs[0][span, :]
+        for ref in inputs[1:]:
+            total = total + ref[span, :]
         out[...] = total
-
-
-def total_kernel(*refs):
-    inputs, out = refs[:-1], refs[-1]
-    total = inputs[0][...]
-    for ref in inputs[1:]:
-        total = total + ref[...]
-    out[...] = total
+        start += out.shape[0]
 
 
 def intensity_kernel(value, *refs):
@@ -210,7 +221,7 @@
     index = lax.broadcasted_iota(jnp.int32, (8, LANES), 1) ^ (mask & (LANES - 1))
     turn = lax.broadcasted_iota(jnp.int32, (8, LANES), 0) ^ (local & 7)
     swap = (mask & LANES) != 0
-    for relative, ref in enumerate(inputs):
+    for relative, ref in zip(UNFOLD_ORDER, inputs):
         base = (relative ^ own) * plan.share
         for group in range(0, plan.share, 8):
             rows = ref[group : group + 8, :]
@@ -242,39 +253,41 @@
         rows, width = first.shape
         return small_call(join_kernel, [(2 * rows, width)], "join", first, second, *order)[0]
 
-    row = plan.sy * plan.sz
+    gather_steps, reduce_steps = plan.steps()
     owner = tile_owner.reshape(1, -1)
     box = tile_box.reshape(1, -1)
     own = accumulate(plan, counts, row_split, col_split, efficiency, lorentz, angles, owner, box)
-    arrived = [swap(array, row, 2 * row) for array in own]
+    arrived = [swap(array, *gather_steps) for array in own]
     held = small_call(stage_kernel, [array.shape for array in own], "stage", *own, flops=LARGE)
     near = [join(held[0], arrived[0])]
     near.append(join(held[1], arrived[1], near[0]))
-    far = [swap(array, 2 * row, row) for array in near]
-    def box_sums(payload, relative, olds, *waits, flops=1):
-        count = plan.sy if relative else 1
-        kernel = functools.partial(scatter_kernel, plan, relative, len(olds), count)
-        shapes = [(row * plan.share // count, VOX)] * count
+    far = [swap(array, *gather_steps[::-1]) for array in near]
+    def box_sums(payload, olds, *waits, flops=1):
+        kernel = functools.partial(scatter_kernel, plan, len(olds), plan.sy)
+        shapes = [(4 * plan.share, VOX)] * plan.sy
         return small_call(kernel, shapes, "box_sums", payload, *olds, *waits, flops=flops)
 
-    def spread(arrived):
-        kernel = functools.partial(split_kernel, plan.sz)
-        parts = small_call(kernel, [(plan.share, VOX)] * plan.sz, "core_sums", *arrived)
-        return parts, [parts[0]] + [swap(parts[i], i) for i in range(1, plan.sz)]
-
-    sums = [box_sums(near[0], True, []), box_sums(near[1], True, [], flops=LARGE)]
-    value = box_sums(far[0], True, sums[0], sums[1][0])
-    weight = box_sums(far[1], True, sums[1], value[0])
-    value = [value[0]] + [swap(value[i], i * plan.sz) for i in range(1, plan.sy)]
-    weight = [weight[0]] + [swap(weight[i], i * plan.sz) for i in range(1, plan.sy)]
-    parts, values = spread(value)
-    _, weights = spread(weight)
-    (value,) = small_call(total_kernel, [(plan.share, VOX)], "value_total", *values, flops=LARGE)
-    (own,) = small_call(intensity_kernel, [(plan.share, VOX)], "intensity", value, *weights)
+    def added(arrays, pieces, flops=1):
+        shape = (arrays[0].shape[0] // pieces, VOX)
+        kernel = functools.partial(add_kernel, len(arrays))
+        return small_call(kernel, [shape] * pieces, "added", *arrays, flops=flops)
+
+    sums = [box_sums(near[0], []), box_sums(near[1], [], flops=LARGE)]
+    value = box_sums(far[0], sums[0], sums[1][0])
+    weight = box_sums(far[1], sums[1], value[0])
+    pairs = []
+    for parts in (value, weight):
+        parts = [parts[0]] + [swap(parts[i], i * plan.sz) for i in range(1, plan.sy)]
+        for even, odd in (reduce_steps, reduce_steps[::-1]):
+            keep, give = added(parts, 2)
+            parts = [keep, swap(give, even, odd)]
+        pairs.append(parts)
+    (value,) = added(pairs[0], 1, flops=LARGE)
+    (own,) = small_call(intensity_kernel, [(plan.share, VOX)], "intensity", value, *pairs[1])
     flip_x, flip_y, flip_z = plan.flip_dev
     near = [own, swap(own, flip_z), swap(own, flip_x), swap(own, flip_x ^ flip_z)]
     far = [swap(array, flip_y) for array in near]
-    ordered = [near[0], near[1], far[0], far[1], near[2], near[3], far[2], far[3]]
+    ordered = [array for pair in zip(near, far) for array in pair][::-1]
     (result,) = small_call(functools.partial(unfold_kernel, plan), [(plan.boxes, VOX)], "unfold", *ordered)
     return result.reshape(GX // plan.sx, GY // plan.sy, GZ // plan.sz, BOX_BRICK, VOX)
 

time: 56.4 us -> 55.9 us (level)
  starting transfers between devices: 22.6 us -> 21.8 us
    ppermute x19 -> x17, starting transfers between devices: 22.6 us -> 21.8 us  [swap(): return lax.ppermute(array, AXES, pairs)]
    ppermute x19 -> x17, waiting for transfers between devices: 19.1 us -> 19.2 us  [swap(): return lax.ppermute(array, AXES, pairs)]
    pallas_call x12 -> x14, Pallas kernels: 2.37 us -> 2.47 us  [small_call(): pl.pallas_call(kernel, out_shape=[jax.ShapeDtypeStruct(shape, jnp.float32...]
  transfers between devices with their start and end apart: 19 -> 17, of which waited for: 9 -> 9; matrix products, arithmetic and copies ran while one was open for 0% -> 0% of each run, Pallas kernels for 2% -> 3%
where the time goes in v1:
time: 55.9 us; the launch traced here: 55.7 us
  starting transfers between devices  21.8 us (39%)
  waiting for transfers between devices  19.2 us (34%)
  Pallas kernels  12.7 us (23%)
  local copies, waits for them, and re-layouts  1.85 us (3%)
    ppermute x17, starting transfers between devices, swap(): return lax.ppermute(array, AXES, pairs)  21.8 us
    ppermute x17, waiting for transfers between devices, swap(): return lax.ppermute(array, AXES, pairs)  19.2 us
    pallas_call x1, Pallas kernels, accumulate(): pl.pallas_call(functools.partial(accumulate_kernel, plan), in_specs=[pl.B...  10.2 us
    pallas_call x14, Pallas kernels, small_call(): pl.pallas_call(kernel, out_shape=[jax.ShapeDtypeStruct(shape, jnp.float32...  2.47 us
    unnamed x4, local copies, waits for them, and re-layouts  1.85 us
  transfers between devices with their start and end apart: 17, of which 9 were waited for; matrix products, arithmetic and copies ran while one was open for 0% of the time, Pallas kernels for 3%

profile of v1, /device:TPU:0, one launch (start us, length us, event | category | flops | bytes accessed | tf_op | source)
XLA Modules:
  0.0 55.7 jit_solution(5920110888217960468)
XLA Ops:
  0.0 10.2 %tile_sums.1 = (f32[136,256]{1,0:T(8,128)}, f32[136,256]{1,0:T(8,128)}) custom-call(s32[2]{0:T(128)} %angles.1, f32[3600]{0:T(1024)} %lorentz.1, s32[1,128]{1,0:T(1,128)} %bitcast.5, s32[1,128]{1,0:T(1,128)} %bitcast.6, bf16[2,64,128,128]{3,2,1,0:T(8,128)(2,1)} %counts.1, bf16[2,64,128,256]{3,2,1,0:T(8,128)(2,1)} %rows.1, bf16[2,64,128,256]{3,2,1,0:T(8,128)(2,1)} %cols.1, ...), custom_call_target="tpu_custom_call" | custom-call | flops 2147483648 | bytes 23068672 | tf_op jit(solution)/shard_map/tile_sums/pallas_call | solution.py:144
  10.2 3.0 %collective-permute-start = (f32[136,256]{1,0:T(8,128)}, f32[136,256]{1,0:T(8,128)S(1)}, u32[]{:S(2)}, u32[]{:S(2)}) collective-permute-start(f32[136,256]{1,0:T(8,128)} %get-tuple-element.25.first), channel_id=1, source_target_pairs={{0,8},{1,9},{2,10},{3,11},{4,5},{5,4},{6,7},{7,6},{8,0},{9,1},{10,... | collective-permute-start | bytes 417800 | tf_op jit(solution)/shard_map/ppermute | solution.py:250
  13.3 0.9 %copy-done = f32[136,256]{1,0:T(8,128)S(1)} copy-done((f32[136,256]{1,0:T(8,128)S(1)}, f32[136,256]{1,0:T(8,128)}, u32[]{:S(2)}) %copy-start) | copy-done | bytes 139288
  14.3 0.9 %copy-done.1 = f32[136,256]{1,0:T(8,128)S(1)} copy-done((f32[136,256]{1,0:T(8,128)S(1)}, f32[136,256]{1,0:T(8,128)}, u32[]{:S(2)}) %copy-start.1) | copy-done | bytes 139288
  15.2 1.3 %collective-permute-done.second = f32[136,256]{1,0:T(8,128)S(1)} collective-permute-done((f32[136,256]{1,0:T(8,128)}, f32[136,256]{1,0:T(8,128)S(1)}, u32[]{:S(2)}, u32[]{:S(2)}) %collective-permute-start) | collective-permute-done | bytes 139296 | tf_op jit(solution)/shard_map/ppermute | solution.py:250
  16.5 2.2 %collective-permute-start.1 = (f32[272,256]{1,0:T(8,128)S(1)}, f32[272,256]{1,0:T(8,128)S(1)}, u32[]{:S(2)}, u32[]{:S(2)}) collective-permute-start(f32[272,256]{1,0:T(8,128)S(1)} %join.2.payload.rest_0_), channel_id=1, source_target_pairs={{0,1},{1,0},{2,3},{3,2},{4,12},{5,13},{6,14},{7,15},{8,9},{9,8},{1... | collective-permute-start | bytes 835592 | tf_op jit(solution)/shard_map/ppermute | solution.py:250
  18.7 1.5 %collective-permute-start.6 = (f32[272,256]{1,0:T(8,128)S(1)}, f32[272,256]{1,0:T(8,128)S(1)}, u32[]{:S(2)}, u32[]{:S(2)}) collective-permute-start(f32[272,256]{1,0:T(8,128)S(1)} %join.3.payload), channel_id=1, source_target_pairs={{0,1},{1,0},{2,3},{3,2},{4,12},{5,13},{6,14},{7,15},{8,9},{9,8},{1... | collective-permute-start | bytes 835592 | tf_op jit(solution)/shard_map/ppermute | solution.py:250
  20.8 2.4 %collective-permute-done.1.payload = f32[272,256]{1,0:T(8,128)S(1)} collective-permute-done((f32[272,256]{1,0:T(8,128)S(1)}, f32[272,256]{1,0:T(8,128)S(1)}, u32[]{:S(2)}, u32[]{:S(2)}) %collective-permute-start.1) | collective-permute-done | bytes 278560 | tf_op jit(solution)/shard_map/ppermute | solution.py:250
  23.6 2.6 %collective-permute-done.6.payload = f32[272,256]{1,0:T(8,128)S(1)} collective-permute-done((f32[272,256]{1,0:T(8,128)S(1)}, f32[272,256]{1,0:T(8,128)S(1)}, u32[]{:S(2)}, u32[]{:S(2)}) %collective-permute-start.6) | collective-permute-done | bytes 278560 | tf_op jit(solution)/shard_map/ppermute | solution.py:250
  26.7 2.0 %collective-permute-start.4 = (f32[128,256]{1,0:T(8,128)S(1)}, f32[128,256]{1,0:T(8,128)S(1)}, u32[]{:S(2)}, u32[]{:S(2)}) collective-permute-start(f32[128,256]{1,0:T(8,128)S(1)} %get-tuple-element.35), channel_id=1, source_target_pairs={{0,16},{1,17},{2,18},{3,19},{4,6},{5,7},{6,4},{7,5},{8,24},{9,25},... | collective-permute-start | bytes 393224 | tf_op jit(solution)/shard_map/ppermute | solution.py:250
  28.7 1.5 %collective-permute-start.8 = (f32[128,256]{1,0:T(8,128)S(1)}, f32[128,256]{1,0:T(8,128)S(1)}, u32[]{:S(2)}, u32[]{:S(2)}) collective-permute-start(f32[128,256]{1,0:T(8,128)S(1)} %get-tuple-element.42), channel_id=1, source_target_pairs={{0,16},{1,17},{2,18},{3,19},{4,6},{5,7},{6,4},{7,5},{8,24},{9,25},... | collective-permute-start | bytes 393224 | tf_op jit(solution)/shard_map/ppermute | solution.py:250
  30.2 1.5 %collective-permute-done.4.refs_1_ = f32[128,256]{1,0:T(8,128)S(1)} collective-permute-done((f32[128,256]{1,0:T(8,128)S(1)}, f32[128,256]{1,0:T(8,128)S(1)}, u32[]{:S(2)}, u32[]{:S(2)}) %collective-permute-start.4) | collective-permute-done | bytes 131104 | tf_op jit(solution)/shard_map/ppermute | solution.py:250
  31.7 3.1 %collective-permute-start.5 = (f32[64,256]{1,0:T(8,128)S(1)}, f32[64,256]{1,0:T(8,128)S(1)}, u32[]{:S(2)}, u32[]{:S(2)}) collective-permute-start(f32[64,256]{1,0:T(8,128)S(1)} %get-tuple-element.37), channel_id=1, source_target_pairs={{0,2},{1,3},{2,0},{3,1},{4,20},{5,21},{6,22},{7,23},{8,10},{9,11},... | collective-permute-start | bytes 196616 | tf_op jit(solution)/shard_map/ppermute | solution.py:250
  34.8 1.6 %collective-permute-start.9 = (f32[64,256]{1,0:T(8,128)S(1)}, f32[64,256]{1,0:T(8,128)S(1)}, u32[]{:S(2)}, u32[]{:S(2)}) collective-permute-start(f32[64,256]{1,0:T(8,128)S(1)} %get-tuple-element.44), channel_id=1, source_target_pairs={{0,2},{1,3},{2,0},{3,1},{4,20},{5,21},{6,22},{7,23},{8,10},{9,11},... | collective-permute-start | bytes 196616 | tf_op jit(solution)/shard_map/ppermute | solution.py:250
  36.4 1.0 %collective-permute-done.5.refs_1_ = f32[64,256]{1,0:T(8,128)S(1)} collective-permute-done((f32[64,256]{1,0:T(8,128)S(1)}, f32[64,256]{1,0:T(8,128)S(1)}, u32[]{:S(2)}, u32[]{:S(2)}) %collective-permute-start.5) | collective-permute-done | bytes 65568 | tf_op jit(solution)/shard_map/ppermute | solution.py:250
  37.4 2.6 %collective-permute-done.9.refs_1_ = f32[64,256]{1,0:T(8,128)S(1)} collective-permute-done((f32[64,256]{1,0:T(8,128)S(1)}, f32[64,256]{1,0:T(8,128)S(1)}, u32[]{:S(2)}, u32[]{:S(2)}) %collective-permute-start.9) | collective-permute-done | bytes 65568 | tf_op jit(solution)/shard_map/ppermute | solution.py:250
  40.1 3.2 %collective-permute-start.14 = (f32[64,256]{1,0:T(8,128)S(1)}, f32[64,256]{1,0:T(8,128)S(1)}, u32[]{:S(2)}, u32[]{:S(2)}) collective-permute-start(f32[64,256]{1,0:T(8,128)S(1)} %intensity.1.refs_7_), channel_id=1, source_target_pairs={{0,3},{1,2},{2,1},{3,0},{4,7},{5,6},{6,5},{7,4},{8,11},{9,10},{10,... | collective-permute-start | bytes 196616 | tf_op jit(solution)/shard_map/ppermute | solution.py:250
  43.3 2.3 %collective-permute-start.12 = (f32[64,256]{1,0:T(8,128)S(1)}, f32[64,256]{1,0:T(8,128)S(1)}, u32[]{:S(2)}, u32[]{:S(2)}) collective-permute-start(f32[64,256]{1,0:T(8,128)S(1)} %intensity.1.refs_7_), channel_id=1, source_target_pairs={{0,24},{1,25},{2,26},{3,27},{4,28},{5,29},{6,30},{7,31},{8,16},{9,... | collective-permute-start | bytes 196616 | tf_op jit(solution)/shard_map/ppermute | solution.py:250
  45.6 0.7 %collective-permute-start.10 = (f32[64,256]{1,0:T(8,128)S(1)}, f32[64,256]{1,0:T(8,128)S(1)}, u32[]{:S(2)}, u32[]{:S(2)}) collective-permute-start(f32[64,256]{1,0:T(8,128)S(1)} %intensity.1.refs_7_), channel_id=1, source_target_pairs={{0,27},{1,26},{2,25},{3,24},{4,31},{5,30},{6,29},{7,28},{8,19},{9,... | collective-permute-start | bytes 196616 | tf_op jit(solution)/shard_map/ppermute | solution.py:250
  46.3 0.5 collective-permute-start.15
  46.9 1.6 %collective-permute-done.12.refs_3_ = f32[64,256]{1,0:T(8,128)S(1)} collective-permute-done((f32[64,256]{1,0:T(8,128)S(1)}, f32[64,256]{1,0:T(8,128)S(1)}, u32[]{:S(2)}, u32[]{:S(2)}) %collective-permute-start.12) | collective-permute-done | bytes 65568 | tf_op jit(solution)/shard_map/ppermute | solution.py:250
  48.4 5.0 %collective-permute-done.10.refs_1_ = f32[64,256]{1,0:T(8,128)S(1)} collective-permute-done((f32[64,256]{1,0:T(8,128)S(1)}, f32[64,256]{1,0:T(8,128)S(1)}, u32[]{:S(2)}, u32[]{:S(2)}) %collective-permute-start.10) | collective-permute-done | bytes 65568 | tf_op jit(solution)/shard_map/ppermute | solution.py:250
  53.5 1.2 %collective-permute-done.11.refs_0_ = f32[64,256]{1,0:T(8,128)S(1)} collective-permute-done((f32[64,256]{1,0:T(8,128)S(1)}, f32[64,256]{1,0:T(8,128)S(1)}, u32[]{:S(2)}, u32[]{:S(2)}) %collective-permute-start.11) | collective-permute-done | bytes 65568 | tf_op jit(solution)/shard_map/ppermute | solution.py:250
  54.7 1.0 %unfold.1 = f32[512,256]{1,0:T(8,128)} custom-call(f32[64,256]{1,0:T(8,128)S(1)} %collective-permute-done.11.refs_0_, f32[64,256]{1,0:T(8,128)S(1)} %collective-permute-done.10.refs_1_, f32[64,256]{1,0:T(8,128)S(1)} %collective-permute-done.13.refs_2_, f32[64,256]{1,0:T(8,128)S(1)} %collective-permute-done.12.refs_3_, ...), custom_call_target="tpu_custom_call" | custom-call | flops 1 | bytes 1 | tf_op jit(solution)/shard_map/unfold/pallas_call | solution.py:237
  (29 shorter events, 1.7 us)
Async XLA Ops:
  10.2 6.2 %collective-permute-start = (f32[136,256]{1,0:T(8,128)}, f32[136,256]{1,0:T(8,128)S(1)}, u32[]{:S(2)}, u32[]{:S(2)}) collective-permute-start(f32[136,256]{1,0:T(8,128)} %get-tuple-element.25.first), channel_id=1, source_target_pairs={{0,8},{1,9},{2,10},{3,11},{4,5},{5,4},{6,7},{7,6},{8,0},{9,1},{10,... | collective-permute-start | bytes 417800 | tf_op jit(solution)/shard_map/ppermute | solution.py:250
  13.2 5.4 %collective-permute-start.2 = (f32[136,256]{1,0:T(8,128)}, f32[136,256]{1,0:T(8,128)S(1)}, u32[]{:S(2)}, u32[]{:S(2)}) collective-permute-start(f32[136,256]{1,0:T(8,128)} %get-tuple-element.26.second), channel_id=1, source_target_pairs={{0,8},{1,9},{2,10},{3,11},{4,5},{5,4},{6,7},{7,6},{8,0},{9,1},{10,... | collective-permute-start | bytes 417800 | tf_op jit(solution)/shard_map/ppermute | solution.py:250
  13.3 0.9 %copy-start = (f32[136,256]{1,0:T(8,128)S(1)}, f32[136,256]{1,0:T(8,128)}, u32[]{:S(2)}) copy-start(f32[136,256]{1,0:T(8,128)} %get-tuple-element.26.second) | copy-start | bytes 417796
  14.3 0.9 %copy-start.1 = (f32[136,256]{1,0:T(8,128)S(1)}, f32[136,256]{1,0:T(8,128)}, u32[]{:S(2)}) copy-start(f32[136,256]{1,0:T(8,128)} %get-tuple-element.25.first) | copy-start | bytes 417796
  16.5 6.7 %collective-permute-start.1 = (f32[272,256]{1,0:T(8,128)S(1)}, f32[272,256]{1,0:T(8,128)S(1)}, u32[]{:S(2)}, u32[]{:S(2)}) collective-permute-start(f32[272,256]{1,0:T(8,128)S(1)} %join.2.payload.rest_0_), channel_id=1, source_target_pairs={{0,1},{1,0},{2,3},{3,2},{4,12},{5,13},{6,14},{7,15},{8,9},{9,8},{1... | collective-permute-start | bytes 835592 | tf_op jit(solution)/shard_map/ppermute | solution.py:250
  18.7 7.5 %collective-permute-start.6 = (f32[272,256]{1,0:T(8,128)S(1)}, f32[272,256]{1,0:T(8,128)S(1)}, u32[]{:S(2)}, u32[]{:S(2)}) collective-permute-start(f32[272,256]{1,0:T(8,128)S(1)} %join.3.payload), channel_id=1, source_target_pairs={{0,1},{1,0},{2,3},{3,2},{4,12},{5,13},{6,14},{7,15},{8,9},{9,8},{1... | collective-permute-start | bytes 835592 | tf_op jit(solution)/shard_map/ppermute | solution.py:250
  23.5 3.1 %collective-permute-start.3 = (f32[256,256]{1,0:T(8,128)S(1)}, f32[256,256]{1,0:T(8,128)S(1)}, u32[]{:S(2)}, u32[]{:S(2)}) collective-permute-start(f32[256,256]{1,0:T(8,128)S(1)} %get-tuple-element.33), channel_id=1, source_target_pairs={{0,4},{1,5},{2,6},{3,7},{4,0},{5,1},{6,2},{7,3},{8,12},{9,13},{10,... | collective-permute-start | bytes 786440 | tf_op jit(solution)/shard_map/ppermute | solution.py:250
  26.5 2.2 %collective-permute-start.7 = (f32[256,256]{1,0:T(8,128)S(1)}, f32[256,256]{1,0:T(8,128)S(1)}, u32[]{:S(2)}, u32[]{:S(2)}) collective-permute-start(f32[256,256]{1,0:T(8,128)S(1)} %get-tuple-element.40), channel_id=1, source_target_pairs={{0,4},{1,5},{2,6},{3,7},{4,0},{5,1},{6,2},{7,3},{8,12},{9,13},{10,... | collective-permute-start | bytes 786440 | tf_op jit(solution)/shard_map/ppermute | solution.py:250
  26.7 5.0 %collective-permute-start.4 = (f32[128,256]{1,0:T(8,128)S(1)}, f32[128,256]{1,0:T(8,128)S(1)}, u32[]{:S(2)}, u32[]{:S(2)}) collective-permute-start(f32[128,256]{1,0:T(8,128)S(1)} %get-tuple-element.35), channel_id=1, source_target_pairs={{0,16},{1,17},{2,18},{3,19},{4,6},{5,7},{6,4},{7,5},{8,24},{9,25},... | collective-permute-start | bytes 393224 | tf_op jit(solution)/shard_map/ppermute | solution.py:250
  28.7 6.1 %collective-permute-start.8 = (f32[128,256]{1,0:T(8,128)S(1)}, f32[128,256]{1,0:T(8,128)S(1)}, u32[]{:S(2)}, u32[]{:S(2)}) collective-permute-start(f32[128,256]{1,0:T(8,128)S(1)} %get-tuple-element.42), channel_id=1, source_target_pairs={{0,16},{1,17},{2,18},{3,19},{4,6},{5,7},{6,4},{7,5},{8,24},{9,25},... | collective-permute-start | bytes 393224 | tf_op jit(solution)/shard_map/ppermute | solution.py:250
  31.7 5.7 %collective-permute-start.5 = (f32[64,256]{1,0:T(8,128)S(1)}, f32[64,256]{1,0:T(8,128)S(1)}, u32[]{:S(2)}, u32[]{:S(2)}) collective-permute-start(f32[64,256]{1,0:T(8,128)S(1)} %get-tuple-element.37), channel_id=1, source_target_pairs={{0,2},{1,3},{2,0},{3,1},{4,20},{5,21},{6,22},{7,23},{8,10},{9,11},... | collective-permute-start | bytes 196616 | tf_op jit(solution)/shard_map/ppermute | solution.py:250
  34.8 5.2 %collective-permute-start.9 = (f32[64,256]{1,0:T(8,128)S(1)}, f32[64,256]{1,0:T(8,128)S(1)}, u32[]{:S(2)}, u32[]{:S(2)}) collective-permute-start(f32[64,256]{1,0:T(8,128)S(1)} %get-tuple-element.44), channel_id=1, source_target_pairs={{0,2},{1,3},{2,0},{3,1},{4,20},{5,21},{6,22},{7,23},{8,10},{9,11},... | collective-permute-start | bytes 196616 | tf_op jit(solution)/shard_map/ppermute | solution.py:250
  40.1 6.3 %collective-permute-start.14 = (f32[64,256]{1,0:T(8,128)S(1)}, f32[64,256]{1,0:T(8,128)S(1)}, u32[]{:S(2)}, u32[]{:S(2)}) collective-permute-start(f32[64,256]{1,0:T(8,128)S(1)} %intensity.1.refs_7_), channel_id=1, source_target_pairs={{0,3},{1,2},{2,1},{3,0},{4,7},{5,6},{6,5},{7,4},{8,11},{9,10},{10,... | collective-permute-start | bytes 196616 | tf_op jit(solution)/shard_map/ppermute | solution.py:250
  43.3 5.2 %collective-permute-start.12 = (f32[64,256]{1,0:T(8,128)S(1)}, f32[64,256]{1,0:T(8,128)S(1)}, u32[]{:S(2)}, u32[]{:S(2)}) collective-permute-start(f32[64,256]{1,0:T(8,128)S(1)} %intensity.1.refs_7_), channel_id=1, source_target_pairs={{0,24},{1,25},{2,26},{3,27},{4,28},{5,29},{6,30},{7,31},{8,16},{9,... | collective-permute-start | bytes 196616 | tf_op jit(solution)/shard_map/ppermute | solution.py:250
  45.6 7.9 %collective-permute-start.10 = (f32[64,256]{1,0:T(8,128)S(1)}, f32[64,256]{1,0:T(8,128)S(1)}, u32[]{:S(2)}, u32[]{:S(2)}) collective-permute-start(f32[64,256]{1,0:T(8,128)S(1)} %intensity.1.refs_7_), channel_id=1, source_target_pairs={{0,27},{1,26},{2,25},{3,24},{4,31},{5,30},{6,29},{7,28},{8,19},{9,... | collective-permute-start | bytes 196616 | tf_op jit(solution)/shard_map/ppermute | solution.py:250
  46.3 7.1 %collective-permute-start.16 = (f32[64,256]{1,0:T(8,128)S(1)}, f32[64,256]{1,0:T(8,128)S(1)}, u32[]{:S(2)}, u32[]{:S(2)}) collective-permute-start(f32[64,256]{1,0:T(8,128)S(1)} %intensity.1.refs_7_), channel_id=1, source_target_pairs={{0,4},{1,5},{2,6},{3,7},{4,0},{5,1},{6,2},{7,3},{8,12},{9,13},{10,... | collective-permute-start | bytes 196616 | tf_op jit(solution)/shard_map/ppermute | solution.py:250
  46.3 7.1 %collective-permute-start.15 = (f32[64,256]{1,0:T(8,128)S(1)}, f32[64,256]{1,0:T(8,128)S(1)}, u32[]{:S(2)}, u32[]{:S(2)}) collective-permute-start(f32[64,256]{1,0:T(8,128)S(1)} %collective-permute-done.14.refs_5_), channel_id=1, source_target_pairs={{0,4},{1,5},{2,6},{3,7},{4,0},{5,1},{6,2},{7,3},{8,12},{9,13},{10,... | collective-permute-start | bytes 196616 | tf_op jit(solution)/shard_map/ppermute | solution.py:250
  48.4 5.0 %collective-permute-start.13 = (f32[64,256]{1,0:T(8,128)S(1)}, f32[64,256]{1,0:T(8,128)S(1)}, u32[]{:S(2)}, u32[]{:S(2)}) collective-permute-start(f32[64,256]{1,0:T(8,128)S(1)} %collective-permute-done.12.refs_3_), channel_id=1, source_target_pairs={{0,4},{1,5},{2,6},{3,7},{4,0},{5,1},{6,2},{7,3},{8,12},{9,13},{10,... | collective-permute-start | bytes 196616 | tf_op jit(solution)/shard_map/ppermute | solution.py:250
  53.5 1.3 %collective-permute-start.11 = (f32[64,256]{1,0:T(8,128)S(1)}, f32[64,256]{1,0:T(8,128)S(1)}, u32[]{:S(2)}, u32[]{:S(2)}) collective-permute-start(f32[64,256]{1,0:T(8,128)S(1)} %collective-permute-done.10.refs_1_), channel_id=1, source_target_pairs={{0,4},{1,5},{2,6},{3,7},{4,0},{5,1},{6,2},{7,3},{8,12},{9,13},{10,... | collective-permute-start | bytes 196616 | tf_op jit(solution)/shard_map/ppermute | solution.py:250

commit v2 on v1

--- a/solution.py
+++ b/solution.py
@@ -20,7 +20,7 @@
 TILE_LIMIT = 56 * 1024 * 1024
 VMEM_LIMIT = 24 * 1024 * 1024
 LARGE = 10**10
-UNFOLD_ORDER = (7, 5, 6, 4, 3, 1, 2, 0)
+PIXEL_ROWS = 64
 
 
 class Plan:
@@ -112,16 +112,19 @@
         lanes = lax.broadcasted_iota(jnp.int32, (POSITIONS, LANES), 1)
         for p in range(POSITIONS):
             at = block * POSITIONS + p
-            cols_all = jnp.concatenate([held_cols[f, at] for f in range(frames)], axis=1)
-            seen_all = jnp.dot(held_seen[at], cols_all, preferred_element_type=jnp.float32)
             for f in range(frames):
-                spread = held_rows[f, at].astype(jnp.float32)
-                counted = jnp.dot(held_counts[f, at], held_cols[f, at], preferred_element_type=jnp.float32)
-                observed = seen_all[:, f * VOX : (f + 1) * VOX]
-                for kind, item in enumerate((counted, observed)):
-                    product = jnp.sum((spread * item).reshape(-1, 8, VOX), axis=0)
-                    partial[f, kind, 0, p * 8 : (p + 1) * 8, :] = product[:, :LANES]
-                    partial[f, kind, 1, p * 8 : (p + 1) * 8, :] = product[:, LANES:]
+                weights = held_cols[f, at]
+                for kind in range(2):
+                    total = None
+                    for start in range(0, held_rows.shape[2], PIXEL_ROWS):
+                        span = pl.ds(start, PIXEL_ROWS)
+                        pixels = held_seen[at, span, :] if kind else held_counts[f, at, span, :]
+                        item = jnp.dot(pixels, weights, preferred_element_type=jnp.float32)
+                        item = held_rows[f, at, span, :].astype(jnp.float32) * item
+                        item = jnp.sum(item.reshape(-1, 8, VOX), axis=0)
+                        total = item if total is None else total + item
+                    partial[f, kind, 0, p * 8 : (p + 1) * 8, :] = total[:, :LANES]
+                    partial[f, kind, 1, p * 8 : (p + 1) * 8, :] = total[:, LANES:]
         for f in range(frames):
             place = pl.ds(pl.multiple_of(f * positions + block * POSITIONS, POSITIONS), POSITIONS)
             mask = jnp.broadcast_to(turned[place, :], (POSITIONS, LANES))
@@ -221,7 +224,7 @@
     index = lax.broadcasted_iota(jnp.int32, (8, LANES), 1) ^ (mask & (LANES - 1))
     turn = lax.broadcasted_iota(jnp.int32, (8, LANES), 0) ^ (local & 7)
     swap = (mask & LANES) != 0
-    for relative, ref in zip(UNFOLD_ORDER, inputs):
+    for relative, ref in enumerate(inputs):
         base = (relative ^ own) * plan.share
         for group in range(0, plan.share, 8):
             rows = ref[group : group + 8, :]
@@ -287,7 +290,7 @@
     flip_x, flip_y, flip_z = plan.flip_dev
     near = [own, swap(own, flip_z), swap(own, flip_x), swap(own, flip_x ^ flip_z)]
     far = [swap(array, flip_y) for array in near]
-    ordered = [array for pair in zip(near, far) for array in pair][::-1]
+    ordered = [near[0], near[1], far[0], far[1], near[2], near[3], far[2], far[3]]
     (result,) = small_call(functools.partial(unfold_kernel, plan), [(plan.boxes, VOX)], "unfold", *ordered)
     return result.reshape(GX // plan.sx, GY // plan.sy, GZ // plan.sz, BOX_BRICK, VOX)
 

time: 55.9 us -> 54.2 us (0.970)
  waiting for transfers between devices: 19.2 us -> 18 us
    ppermute x17, waiting for transfers between devices: 19.2 us -> 18 us  [swap(): return lax.ppermute(array, AXES, pairs)]
  transfers between devices with their start and end apart: 17 -> 17, of which waited for: 9 -> 10; matrix products, arithmetic and copies ran while one was open for 0% -> 0% of each run, Pallas kernels for 3% -> 3%
where the time goes in v2:
time: 54.2 us; the launch traced here: 53.9 us
  starting transfers between devices  21.3 us (39%)
  waiting for transfers between devices  18 us (33%)
  Pallas kernels  12.7 us (23%)
  local copies, waits for them, and re-layouts  1.85 us (3%)
    ppermute x17, starting transfers between devices, swap(): return lax.ppermute(array, AXES, pairs)  21.3 us
    ppermute x17, waiting for transfers between devices, swap(): return lax.ppermute(array, AXES, pairs)  18 us
    pallas_call x1, Pallas kernels, accumulate(): pl.pallas_call(functools.partial(accumulate_kernel, plan), in_specs=[pl.B...  10.2 us
    pallas_call x14, Pallas kernels, small_call(): pl.pallas_call(kernel, out_shape=[jax.ShapeDtypeStruct(shape, jnp.float32...  2.47 us
    unnamed x4, local copies, waits for them, and re-layouts  1.85 us
  transfers between devices with their start and end apart: 17, of which 10 were waited for; matrix products, arithmetic and copies ran while one was open for 0% of the time, Pallas kernels for 3%

profile of v2, /device:TPU:0, one launch (start us, length us, event | category | flops | bytes accessed | tf_op | source)
XLA Modules:
  0.0 53.9 jit_solution(8553277092680387693)
XLA Ops:
  0.0 10.2 %tile_sums.1 = (f32[136,256]{1,0:T(8,128)}, f32[136,256]{1,0:T(8,128)}) custom-call(s32[2]{0:T(128)} %angles.1, f32[3600]{0:T(1024)} %lorentz.1, s32[1,128]{1,0:T(1,128)} %bitcast.5, s32[1,128]{1,0:T(1,128)} %bitcast.6, bf16[2,64,128,128]{3,2,1,0:T(8,128)(2,1)} %counts.1, bf16[2,64,128,256]{3,2,1,0:T(8,128)(2,1)} %rows.1, bf16[2,64,128,256]{3,2,1,0:T(8,128)(2,1)} %cols.1, ...), custom_call_target="tpu_custom_call" | custom-call | flops 2147483648 | bytes 23068672 | tf_op jit(solution)/shard_map/tile_sums/pallas_call | solution.py:147
  10.2 3.0 %collective-permute-start = (f32[136,256]{1,0:T(8,128)}, f32[136,256]{1,0:T(8,128)S(1)}, u32[]{:S(2)}, u32[]{:S(2)}) collective-permute-start(f32[136,256]{1,0:T(8,128)} %get-tuple-element.25.first), channel_id=1, source_target_pairs={{0,8},{1,9},{2,10},{3,11},{4,5},{5,4},{6,7},{7,6},{8,0},{9,1},{10,... | collective-permute-start | bytes 417800 | tf_op jit(solution)/shard_map/ppermute | solution.py:253
  13.3 0.9 %copy-done = f32[136,256]{1,0:T(8,128)S(1)} copy-done((f32[136,256]{1,0:T(8,128)S(1)}, f32[136,256]{1,0:T(8,128)}, u32[]{:S(2)}) %copy-start) | copy-done | bytes 139288
  14.2 0.9 %copy-done.1 = f32[136,256]{1,0:T(8,128)S(1)} copy-done((f32[136,256]{1,0:T(8,128)S(1)}, f32[136,256]{1,0:T(8,128)}, u32[]{:S(2)}) %copy-start.1) | copy-done | bytes 139288
  15.2 1.3 %collective-permute-done.second = f32[136,256]{1,0:T(8,128)S(1)} collective-permute-done((f32[136,256]{1,0:T(8,128)}, f32[136,256]{1,0:T(8,128)S(1)}, u32[]{:S(2)}, u32[]{:S(2)}) %collective-permute-start) | collective-permute-done | bytes 139296 | tf_op jit(solution)/shard_map/ppermute | solution.py:253
  16.5 2.2 %collective-permute-start.1 = (f32[272,256]{1,0:T(8,128)S(1)}, f32[272,256]{1,0:T(8,128)S(1)}, u32[]{:S(2)}, u32[]{:S(2)}) collective-permute-start(f32[272,256]{1,0:T(8,128)S(1)} %join.2.payload.rest_0_), channel_id=1, source_target_pairs={{0,1},{1,0},{2,3},{3,2},{4,12},{5,13},{6,14},{7,15},{8,9},{9,8},{1... | collective-permute-start | bytes 835592 | tf_op jit(solution)/shard_map/ppermute | solution.py:253
  18.7 1.5 %collective-permute-start.6 = (f32[272,256]{1,0:T(8,128)S(1)}, f32[272,256]{1,0:T(8,128)S(1)}, u32[]{:S(2)}, u32[]{:S(2)}) collective-permute-start(f32[272,256]{1,0:T(8,128)S(1)} %join.3.payload), channel_id=1, source_target_pairs={{0,1},{1,0},{2,3},{3,2},{4,12},{5,13},{6,14},{7,15},{8,9},{9,8},{1... | collective-permute-start | bytes 835592 | tf_op jit(solution)/shard_map/ppermute | solution.py:253
  20.8 2.4 %collective-permute-done.1.payload = f32[272,256]{1,0:T(8,128)S(1)} collective-permute-done((f32[272,256]{1,0:T(8,128)S(1)}, f32[272,256]{1,0:T(8,128)S(1)}, u32[]{:S(2)}, u32[]{:S(2)}) %collective-permute-start.1) | collective-permute-done | bytes 278560 | tf_op jit(solution)/shard_map/ppermute | solution.py:253
  23.6 2.6 %collective-permute-done.6.payload = f32[272,256]{1,0:T(8,128)S(1)} collective-permute-done((f32[272,256]{1,0:T(8,128)S(1)}, f32[272,256]{1,0:T(8,128)S(1)}, u32[]{:S(2)}, u32[]{:S(2)}) %collective-permute-start.6) | collective-permute-done | bytes 278560 | tf_op jit(solution)/shard_map/ppermute | solution.py:253
  26.6 2.0 %collective-permute-start.4 = (f32[128,256]{1,0:T(8,128)S(1)}, f32[128,256]{1,0:T(8,128)S(1)}, u32[]{:S(2)}, u32[]{:S(2)}) collective-permute-start(f32[128,256]{1,0:T(8,128)S(1)} %get-tuple-element.35), channel_id=1, source_target_pairs={{0,16},{1,17},{2,18},{3,19},{4,6},{5,7},{6,4},{7,5},{8,24},{9,25},... | collective-permute-start | bytes 393224 | tf_op jit(solution)/shard_map/ppermute | solution.py:253
  28.7 1.5 %collective-permute-start.8 = (f32[128,256]{1,0:T(8,128)S(1)}, f32[128,256]{1,0:T(8,128)S(1)}, u32[]{:S(2)}, u32[]{:S(2)}) collective-permute-start(f32[128,256]{1,0:T(8,128)S(1)} %get-tuple-element.42), channel_id=1, source_target_pairs={{0,16},{1,17},{2,18},{3,19},{4,6},{5,7},{6,4},{7,5},{8,24},{9,25},... | collective-permute-start | bytes 393224 | tf_op jit(solution)/shard_map/ppermute | solution.py:253
  30.2 1.5 %collective-permute-done.4.refs_1_ = f32[128,256]{1,0:T(8,128)S(1)} collective-permute-done((f32[128,256]{1,0:T(8,128)S(1)}, f32[128,256]{1,0:T(8,128)S(1)}, u32[]{:S(2)}, u32[]{:S(2)}) %collective-permute-start.4) | collective-permute-done | bytes 131104 | tf_op jit(solution)/shard_map/ppermute | solution.py:253
  31.7 3.1 %collective-permute-start.5 = (f32[64,256]{1,0:T(8,128)S(1)}, f32[64,256]{1,0:T(8,128)S(1)}, u32[]{:S(2)}, u32[]{:S(2)}) collective-permute-start(f32[64,256]{1,0:T(8,128)S(1)} %get-tuple-element.37), channel_id=1, source_target_pairs={{0,2},{1,3},{2,0},{3,1},{4,20},{5,21},{6,22},{7,23},{8,10},{9,11},... | collective-permute-start | bytes 196616 | tf_op jit(solution)/shard_map/ppermute | solution.py:253
  34.8 1.6 %collective-permute-start.9 = (f32[64,256]{1,0:T(8,128)S(1)}, f32[64,256]{1,0:T(8,128)S(1)}, u32[]{:S(2)}, u32[]{:S(2)}) collective-permute-start(f32[64,256]{1,0:T(8,128)S(1)} %get-tuple-element.44), channel_id=1, source_target_pairs={{0,2},{1,3},{2,0},{3,1},{4,20},{5,21},{6,22},{7,23},{8,10},{9,11},... | collective-permute-start | bytes 196616 | tf_op jit(solution)/shard_map/ppermute | solution.py:253
  36.4 1.0 %collective-permute-done.5.refs_1_ = f32[64,256]{1,0:T(8,128)S(1)} collective-permute-done((f32[64,256]{1,0:T(8,128)S(1)}, f32[64,256]{1,0:T(8,128)S(1)}, u32[]{:S(2)}, u32[]{:S(2)}) %collective-permute-start.5) | collective-permute-done | bytes 65568 | tf_op jit(solution)/shard_map/ppermute | solution.py:253
  37.4 2.6 %collective-permute-done.9.refs_1_ = f32[64,256]{1,0:T(8,128)S(1)} collective-permute-done((f32[64,256]{1,0:T(8,128)S(1)}, f32[64,256]{1,0:T(8,128)S(1)}, u32[]{:S(2)}, u32[]{:S(2)}) %collective-permute-start.9) | collective-permute-done | bytes 65568 | tf_op jit(solution)/shard_map/ppermute | solution.py:253
  40.1 5.0 %collective-permute-start.14 = (f32[64,256]{1,0:T(8,128)S(1)}, f32[64,256]{1,0:T(8,128)S(1)}, u32[]{:S(2)}, u32[]{:S(2)}) collective-permute-start(f32[64,256]{1,0:T(8,128)S(1)} %intensity.1.refs_0_), channel_id=1, source_target_pairs={{0,27},{1,26},{2,25},{3,24},{4,31},{5,30},{6,29},{7,28},{8,19},{9,... | collective-permute-start | bytes 196616 | tf_op jit(solution)/shard_map/ppermute | solution.py:253
  45.0 0.6 %collective-permute-start.13 = (f32[64,256]{1,0:T(8,128)S(1)}, f32[64,256]{1,0:T(8,128)S(1)}, u32[]{:S(2)}, u32[]{:S(2)}) collective-permute-start(f32[64,256]{1,0:T(8,128)S(1)} %intensity.1.refs_0_), channel_id=1, source_target_pairs={{0,24},{1,25},{2,26},{3,27},{4,28},{5,29},{6,30},{7,31},{8,16},{9,... | collective-permute-start | bytes 196616 | tf_op jit(solution)/shard_map/ppermute | solution.py:253
  45.6 0.7 %collective-permute-start.10 = (f32[64,256]{1,0:T(8,128)S(1)}, f32[64,256]{1,0:T(8,128)S(1)}, u32[]{:S(2)}, u32[]{:S(2)}) collective-permute-start(f32[64,256]{1,0:T(8,128)S(1)} %intensity.1.refs_0_), channel_id=1, source_target_pairs={{0,3},{1,2},{2,1},{3,0},{4,7},{5,6},{6,5},{7,4},{8,11},{9,10},{10,... | collective-permute-start | bytes 196616 | tf_op jit(solution)/shard_map/ppermute | solution.py:253
  46.3 1.8 %collective-permute-done.14.refs_5_ = f32[64,256]{1,0:T(8,128)S(1)} collective-permute-done((f32[64,256]{1,0:T(8,128)S(1)}, f32[64,256]{1,0:T(8,128)S(1)}, u32[]{:S(2)}, u32[]{:S(2)}) %collective-permute-start.14) | collective-permute-done | bytes 65568 | tf_op jit(solution)/shard_map/ppermute | solution.py:253
  48.1 2.1 %collective-permute-done.13.refs_4_ = f32[64,256]{1,0:T(8,128)S(1)} collective-permute-done((f32[64,256]{1,0:T(8,128)S(1)}, f32[64,256]{1,0:T(8,128)S(1)}, u32[]{:S(2)}, u32[]{:S(2)}) %collective-permute-start.13) | collective-permute-done | bytes 65568 | tf_op jit(solution)/shard_map/ppermute | solution.py:253
  50.2 1.5 %collective-permute-done.10.refs_1_ = f32[64,256]{1,0:T(8,128)S(1)} collective-permute-done((f32[64,256]{1,0:T(8,128)S(1)}, f32[64,256]{1,0:T(8,128)S(1)}, u32[]{:S(2)}, u32[]{:S(2)}) %collective-permute-start.10) | collective-permute-done | bytes 65568 | tf_op jit(solution)/shard_map/ppermute | solution.py:253
  51.7 1.2 %collective-permute-done.12.refs_3_ = f32[64,256]{1,0:T(8,128)S(1)} collective-permute-done((f32[64,256]{1,0:T(8,128)S(1)}, f32[64,256]{1,0:T(8,128)S(1)}, u32[]{:S(2)}, u32[]{:S(2)}) %collective-permute-start.12) | collective-permute-done | bytes 65568 | tf_op jit(solution)/shard_map/ppermute | solution.py:253
  52.9 1.0 %unfold.1 = f32[512,256]{1,0:T(8,128)} custom-call(f32[64,256]{1,0:T(8,128)S(1)} %intensity.1.refs_0_, f32[64,256]{1,0:T(8,128)S(1)} %collective-permute-done.10.refs_1_, f32[64,256]{1,0:T(8,128)S(1)} %collective-permute-done.11.refs_2_, f32[64,256]{1,0:T(8,128)S(1)} %collective-permute-done.12.refs_3_, f32[64,256]{1,0:T(8,128)S(1)} %collective-permute-done.13.refs_4_, ...), custom_call_target="tpu_custom_call" | custom-call | flops 1 | bytes 1 | tf_op jit(solution)/shard_map/unfold/pallas_call | solution.py:240
  (29 shorter events, 1.7 us)
Async XLA Ops:
  10.2 6.2 %collective-permute-start = (f32[136,256]{1,0:T(8,128)}, f32[136,256]{1,0:T(8,128)S(1)}, u32[]{:S(2)}, u32[]{:S(2)}) collective-permute-start(f32[136,256]{1,0:T(8,128)} %get-tuple-element.25.first), channel_id=1, source_target_pairs={{0,8},{1,9},{2,10},{3,11},{4,5},{5,4},{6,7},{7,6},{8,0},{9,1},{10,... | collective-permute-start | bytes 417800 | tf_op jit(solution)/shard_map/ppermute | solution.py:253
  13.2 5.4 %collective-permute-start.2 = (f32[136,256]{1,0:T(8,128)}, f32[136,256]{1,0:T(8,128)S(1)}, u32[]{:S(2)}, u32[]{:S(2)}) collective-permute-start(f32[136,256]{1,0:T(8,128)} %get-tuple-element.26.second), channel_id=1, source_target_pairs={{0,8},{1,9},{2,10},{3,11},{4,5},{5,4},{6,7},{7,6},{8,0},{9,1},{10,... | collective-permute-start | bytes 417800 | tf_op jit(solution)/shard_map/ppermute | solution.py:253
  13.3 0.9 %copy-start = (f32[136,256]{1,0:T(8,128)S(1)}, f32[136,256]{1,0:T(8,128)}, u32[]{:S(2)}) copy-start(f32[136,256]{1,0:T(8,128)} %get-tuple-element.26.second) | copy-start | bytes 417796
  14.2 0.9 %copy-start.1 = (f32[136,256]{1,0:T(8,128)S(1)}, f32[136,256]{1,0:T(8,128)}, u32[]{:S(2)}) copy-start(f32[136,256]{1,0:T(8,128)} %get-tuple-element.25.first) | copy-start | bytes 417796
  16.5 6.7 %collective-permute-start.1 = (f32[272,256]{1,0:T(8,128)S(1)}, f32[272,256]{1,0:T(8,128)S(1)}, u32[]{:S(2)}, u32[]{:S(2)}) collective-permute-start(f32[272,256]{1,0:T(8,128)S(1)} %join.2.payload.rest_0_), channel_id=1, source_target_pairs={{0,1},{1,0},{2,3},{3,2},{4,12},{5,13},{6,14},{7,15},{8,9},{9,8},{1... | collective-permute-start | bytes 835592 | tf_op jit(solution)/shard_map/ppermute | solution.py:253
  18.7 7.5 %collective-permute-start.6 = (f32[272,256]{1,0:T(8,128)S(1)}, f32[272,256]{1,0:T(8,128)S(1)}, u32[]{:S(2)}, u32[]{:S(2)}) collective-permute-start(f32[272,256]{1,0:T(8,128)S(1)} %join.3.payload), channel_id=1, source_target_pairs={{0,1},{1,0},{2,3},{3,2},{4,12},{5,13},{6,14},{7,15},{8,9},{9,8},{1... | collective-permute-start | bytes 835592 | tf_op jit(solution)/shard_map/ppermute | solution.py:253
  23.5 3.1 %collective-permute-start.3 = (f32[256,256]{1,0:T(8,128)S(1)}, f32[256,256]{1,0:T(8,128)S(1)}, u32[]{:S(2)}, u32[]{:S(2)}) collective-permute-start(f32[256,256]{1,0:T(8,128)S(1)} %get-tuple-element.33), channel_id=1, source_target_pairs={{0,4},{1,5},{2,6},{3,7},{4,0},{5,1},{6,2},{7,3},{8,12},{9,13},{10,... | collective-permute-start | bytes 786440 | tf_op jit(solution)/shard_map/ppermute | solution.py:253
  26.5 2.2 %collective-permute-start.7 = (f32[256,256]{1,0:T(8,128)S(1)}, f32[256,256]{1,0:T(8,128)S(1)}, u32[]{:S(2)}, u32[]{:S(2)}) collective-permute-start(f32[256,256]{1,0:T(8,128)S(1)} %get-tuple-element.40), channel_id=1, source_target_pairs={{0,4},{1,5},{2,6},{3,7},{4,0},{5,1},{6,2},{7,3},{8,12},{9,13},{10,... | collective-permute-start | bytes 786440 | tf_op jit(solution)/shard_map/ppermute | solution.py:253
  26.6 5.0 %collective-permute-start.4 = (f32[128,256]{1,0:T(8,128)S(1)}, f32[128,256]{1,0:T(8,128)S(1)}, u32[]{:S(2)}, u32[]{:S(2)}) collective-permute-start(f32[128,256]{1,0:T(8,128)S(1)} %get-tuple-element.35), channel_id=1, source_target_pairs={{0,16},{1,17},{2,18},{3,19},{4,6},{5,7},{6,4},{7,5},{8,24},{9,25},... | collective-permute-start | bytes 393224 | tf_op jit(solution)/shard_map/ppermute | solution.py:253
  28.7 6.1 %collective-permute-start.8 = (f32[128,256]{1,0:T(8,128)S(1)}, f32[128,256]{1,0:T(8,128)S(1)}, u32[]{:S(2)}, u32[]{:S(2)}) collective-permute-start(f32[128,256]{1,0:T(8,128)S(1)} %get-tuple-element.42), channel_id=1, source_target_pairs={{0,16},{1,17},{2,18},{3,19},{4,6},{5,7},{6,4},{7,5},{8,24},{9,25},... | collective-permute-start | bytes 393224 | tf_op jit(solution)/shard_map/ppermute | solution.py:253
  31.7 5.7 %collective-permute-start.5 = (f32[64,256]{1,0:T(8,128)S(1)}, f32[64,256]{1,0:T(8,128)S(1)}, u32[]{:S(2)}, u32[]{:S(2)}) collective-permute-start(f32[64,256]{1,0:T(8,128)S(1)} %get-tuple-element.37), channel_id=1, source_target_pairs={{0,2},{1,3},{2,0},{3,1},{4,20},{5,21},{6,22},{7,23},{8,10},{9,11},... | collective-permute-start | bytes 196616 | tf_op jit(solution)/shard_map/ppermute | solution.py:253
  34.8 5.2 %collective-permute-start.9 = (f32[64,256]{1,0:T(8,128)S(1)}, f32[64,256]{1,0:T(8,128)S(1)}, u32[]{:S(2)}, u32[]{:S(2)}) collective-permute-start(f32[64,256]{1,0:T(8,128)S(1)} %get-tuple-element.44), channel_id=1, source_target_pairs={{0,2},{1,3},{2,0},{3,1},{4,20},{5,21},{6,22},{7,23},{8,10},{9,11},... | collective-permute-start | bytes 196616 | tf_op jit(solution)/shard_map/ppermute | solution.py:253
  40.1 8.0 %collective-permute-start.14 = (f32[64,256]{1,0:T(8,128)S(1)}, f32[64,256]{1,0:T(8,128)S(1)}, u32[]{:S(2)}, u32[]{:S(2)}) collective-permute-start(f32[64,256]{1,0:T(8,128)S(1)} %intensity.1.refs_0_), channel_id=1, source_target_pairs={{0,27},{1,26},{2,25},{3,24},{4,31},{5,30},{6,29},{7,28},{8,19},{9,... | collective-permute-start | bytes 196616 | tf_op jit(solution)/shard_map/ppermute | solution.py:253
  45.0 5.2 %collective-permute-start.13 = (f32[64,256]{1,0:T(8,128)S(1)}, f32[64,256]{1,0:T(8,128)S(1)}, u32[]{:S(2)}, u32[]{:S(2)}) collective-permute-start(f32[64,256]{1,0:T(8,128)S(1)} %intensity.1.refs_0_), channel_id=1, source_target_pairs={{0,24},{1,25},{2,26},{3,27},{4,28},{5,29},{6,30},{7,31},{8,16},{9,... | collective-permute-start | bytes 196616 | tf_op jit(solution)/shard_map/ppermute | solution.py:253
  45.6 6.1 %collective-permute-start.10 = (f32[64,256]{1,0:T(8,128)S(1)}, f32[64,256]{1,0:T(8,128)S(1)}, u32[]{:S(2)}, u32[]{:S(2)}) collective-permute-start(f32[64,256]{1,0:T(8,128)S(1)} %intensity.1.refs_0_), channel_id=1, source_target_pairs={{0,3},{1,2},{2,1},{3,0},{4,7},{5,6},{6,5},{7,4},{8,11},{9,10},{10,... | collective-permute-start | bytes 196616 | tf_op jit(solution)/shard_map/ppermute | solution.py:253
  46.3 5.4 %collective-permute-start.11 = (f32[64,256]{1,0:T(8,128)S(1)}, f32[64,256]{1,0:T(8,128)S(1)}, u32[]{:S(2)}, u32[]{:S(2)}) collective-permute-start(f32[64,256]{1,0:T(8,128)S(1)} %intensity.1.refs_0_), channel_id=1, source_target_pairs={{0,4},{1,5},{2,6},{3,7},{4,0},{5,1},{6,2},{7,3},{8,12},{9,13},{10,... | collective-permute-start | bytes 196616 | tf_op jit(solution)/shard_map/ppermute | solution.py:253
  48.1 3.6 %collective-permute-start.16 = (f32[64,256]{1,0:T(8,128)S(1)}, f32[64,256]{1,0:T(8,128)S(1)}, u32[]{:S(2)}, u32[]{:S(2)}) collective-permute-start(f32[64,256]{1,0:T(8,128)S(1)} %collective-permute-done.14.refs_5_), channel_id=1, source_target_pairs={{0,4},{1,5},{2,6},{3,7},{4,0},{5,1},{6,2},{7,3},{8,12},{9,13},{10,... | collective-permute-start | bytes 196616 | tf_op jit(solution)/shard_map/ppermute | solution.py:253
  50.2 1.5 %collective-permute-start.15 = (f32[64,256]{1,0:T(8,128)S(1)}, f32[64,256]{1,0:T(8,128)S(1)}, u32[]{:S(2)}, u32[]{:S(2)}) collective-permute-start(f32[64,256]{1,0:T(8,128)S(1)} %collective-permute-done.13.refs_4_), channel_id=1, source_target_pairs={{0,4},{1,5},{2,6},{3,7},{4,0},{5,1},{6,2},{7,3},{8,12},{9,13},{10,... | collective-permute-start | bytes 196616 | tf_op jit(solution)/shard_map/ppermute | solution.py:253
  51.7 1.3 %collective-permute-start.12 = (f32[64,256]{1,0:T(8,128)S(1)}, f32[64,256]{1,0:T(8,128)S(1)}, u32[]{:S(2)}, u32[]{:S(2)}) collective-permute-start(f32[64,256]{1,0:T(8,128)S(1)} %collective-permute-done.10.refs_1_), channel_id=1, source_target_pairs={{0,4},{1,5},{2,6},{3,7},{4,0},{5,1},{6,2},{7,3},{8,12},{9,13},{10,... | collective-permute-start | bytes 196616 | tf_op jit(solution)/shard_map/ppermute | solution.py:253

commit v3 on v2

--- a/solution.py
+++ b/solution.py
@@ -92,7 +92,7 @@
 
     for block in range(blocks):
         for copy in copies(block):
-            copy.start()
+            copy.start(priority=1 if block == 0 else 0)
 
     tiles = frames * positions
     across = lax.broadcasted_iota(jnp.int32, (tiles, tiles), 1)
@@ -104,12 +104,9 @@
         out[tiles : tiles + 8, :] = jnp.zeros((8, VOX), jnp.float32)
         out[tiles : tiles + 8, :tiles] = jnp.broadcast_to(ids.astype(jnp.float32), (8, tiles))
 
-    @pl.loop(0, blocks)
-    def _(block):
-        for copy in copies(block):
-            copy.wait()
-        held_counts, held_rows, held_cols, held_seen = arrays
-        lanes = lax.broadcasted_iota(jnp.int32, (POSITIONS, LANES), 1)
+    held_counts, held_rows, held_cols, held_seen = arrays
+
+    def compute(block):
         for p in range(POSITIONS):
             at = block * POSITIONS + p
             for f in range(frames):
@@ -125,6 +122,9 @@
                         total = item if total is None else total + item
                     partial[f, kind, 0, p * 8 : (p + 1) * 8, :] = total[:, :LANES]
                     partial[f, kind, 1, p * 8 : (p + 1) * 8, :] = total[:, LANES:]
+
+    def finish(block):
+        lanes = lax.broadcasted_iota(jnp.int32, (POSITIONS, LANES), 1)
         for f in range(frames):
             place = pl.ds(pl.multiple_of(f * positions + block * POSITIONS, POSITIONS), POSITIONS)
             mask = jnp.broadcast_to(turned[place, :], (POSITIONS, LANES))
@@ -138,6 +138,17 @@
                 scale = lorentz[angles[f]] if kind == 0 else 1.0
                 out[place, :LANES] = lane_gather(jnp.where(swap, high, low), index) * scale
                 out[place, LANES:] = lane_gather(jnp.where(swap, low, high), index) * scale
+
+    partial[...] = jnp.zeros_like(partial)
+
+    @pl.loop(0, blocks)
+    def _(block):
+        for copy in copies(block):
+            copy.wait()
+        finish(jnp.maximum(block - 1, 0))
+        compute(block)
+
+    finish(blocks - 1)
 
 
 def accumulate(plan, counts, row_split, col_split, efficiency, lorentz, angles, owner, box):
@@ -276,10 +287,10 @@
         return small_call(kernel, [shape] * pieces, "added", *arrays, flops=flops)
 
     sums = [box_sums(near[0], []), box_sums(near[1], [], flops=LARGE)]
-    value = box_sums(far[0], sums[0], sums[1][0])
-    weight = box_sums(far[1], sums[1], value[0])
-    pairs = []
-    for parts in (value, weight):
+    pairs, waits = [], [sums[1][0]]
+    for kind in range(2):
+        parts = box_sums(far[kind], sums[kind], *waits, flops=LARGE if kind else 1)
+        waits = [parts[0]]
         parts = [parts[0]] + [swap(parts[i], i * plan.sz) for i in range(1, plan.sy)]
         for even, odd in (reduce_steps, reduce_steps[::-1]):
             keep, give = added(parts, 2)

time: 54.2 us -> 59.3 us (1.094)
  Pallas kernels: 12.7 us -> 17.9 us
    pallas_call x1, Pallas kernels: 10.2 us -> 15.4 us  [accumulate(): pl.pallas_call(functools.partial(accumulate_kernel, plan), in_specs=[pl.B...]
  transfers between devices with their start and end apart: 17 -> 17, of which waited for: 10 -> 10; matrix products, arithmetic and copies ran while one was open for 0% -> 0% of each run, Pallas kernels for 3% -> 2%
where the time goes in v3:
time: 59.3 us; the launch traced here: 59.1 us
  starting transfers between devices  21.3 us (36%)
  waiting for transfers between devices  18 us (30%)
  Pallas kernels  17.9 us (30%)
  local copies, waits for them, and re-layouts  1.85 us (3%)
    ppermute x17, starting transfers between devices, swap(): return lax.ppermute(array, AXES, pairs)  21.3 us
    ppermute x17, waiting for transfers between devices, swap(): return lax.ppermute(array, AXES, pairs)  18 us
    pallas_call x1, Pallas kernels, accumulate(): pl.pallas_call(functools.partial(accumulate_kernel, plan), in_specs=[pl.B...  15.4 us
    pallas_call x14, Pallas kernels, small_call(): pl.pallas_call(kernel, out_shape=[jax.ShapeDtypeStruct(shape, jnp.float32...  2.47 us
    unnamed x4, local copies, waits for them, and re-layouts  1.85 us
  transfers between devices with their start and end apart: 17, of which 10 were waited for; matrix products, arithmetic and copies ran while one was open for 0% of the time, Pallas kernels for 2%

profile of v3, /device:TPU:0, one launch (start us, length us, event | category | flops | bytes accessed | tf_op | source)
XLA Modules:
  0.0 59.1 jit_solution(13809513453686190143)
XLA Ops:
  0.0 15.4 %tile_sums.1 = (f32[136,256]{1,0:T(8,128)}, f32[136,256]{1,0:T(8,128)}) custom-call(s32[2]{0:T(128)} %angles.1, f32[3600]{0:T(1024)} %lorentz.1, s32[1,128]{1,0:T(1,128)} %bitcast.5, s32[1,128]{1,0:T(1,128)} %bitcast.6, bf16[2,64,128,128]{3,2,1,0:T(8,128)(2,1)} %counts.1, bf16[2,64,128,256]{3,2,1,0:T(8,128)(2,1)} %rows.1, bf16[2,64,128,256]{3,2,1,0:T(8,128)(2,1)} %cols.1, ...), custom_call_target="tpu_custom_call" | custom-call | flops 2147483648 | bytes 23068672 | tf_op jit(solution)/shard_map/tile_sums/pallas_call | solution.py:158
  15.4 3.0 %collective-permute-start = (f32[136,256]{1,0:T(8,128)}, f32[136,256]{1,0:T(8,128)S(1)}, u32[]{:S(2)}, u32[]{:S(2)}) collective-permute-start(f32[136,256]{1,0:T(8,128)} %get-tuple-element.25.first), channel_id=1, source_target_pairs={{0,8},{1,9},{2,10},{3,11},{4,5},{5,4},{6,7},{7,6},{8,0},{9,1},{10,... | collective-permute-start | bytes 417800 | tf_op jit(solution)/shard_map/ppermute | solution.py:264
  18.5 0.9 %copy-done = f32[136,256]{1,0:T(8,128)S(1)} copy-done((f32[136,256]{1,0:T(8,128)S(1)}, f32[136,256]{1,0:T(8,128)}, u32[]{:S(2)}) %copy-start) | copy-done | bytes 139288
  19.4 0.9 %copy-done.1 = f32[136,256]{1,0:T(8,128)S(1)} copy-done((f32[136,256]{1,0:T(8,128)S(1)}, f32[136,256]{1,0:T(8,128)}, u32[]{:S(2)}) %copy-start.1) | copy-done | bytes 139288
  20.3 1.3 %collective-permute-done.second = f32[136,256]{1,0:T(8,128)S(1)} collective-permute-done((f32[136,256]{1,0:T(8,128)}, f32[136,256]{1,0:T(8,128)S(1)}, u32[]{:S(2)}, u32[]{:S(2)}) %collective-permute-start) | collective-permute-done | bytes 139296 | tf_op jit(solution)/shard_map/ppermute | solution.py:264
  21.6 2.2 %collective-permute-start.1 = (f32[272,256]{1,0:T(8,128)S(1)}, f32[272,256]{1,0:T(8,128)S(1)}, u32[]{:S(2)}, u32[]{:S(2)}) collective-permute-start(f32[272,256]{1,0:T(8,128)S(1)} %join.2.payload.rest_0_), channel_id=1, source_target_pairs={{0,1},{1,0},{2,3},{3,2},{4,12},{5,13},{6,14},{7,15},{8,9},{9,8},{1... | collective-permute-start | bytes 835592 | tf_op jit(solution)/shard_map/ppermute | solution.py:264
  23.9 1.5 %collective-permute-start.6 = (f32[272,256]{1,0:T(8,128)S(1)}, f32[272,256]{1,0:T(8,128)S(1)}, u32[]{:S(2)}, u32[]{:S(2)}) collective-permute-start(f32[272,256]{1,0:T(8,128)S(1)} %join.3.payload), channel_id=1, source_target_pairs={{0,1},{1,0},{2,3},{3,2},{4,12},{5,13},{6,14},{7,15},{8,9},{9,8},{1... | collective-permute-start | bytes 835592 | tf_op jit(solution)/shard_map/ppermute | solution.py:264
  26.0 2.4 %collective-permute-done.1.payload = f32[272,256]{1,0:T(8,128)S(1)} collective-permute-done((f32[272,256]{1,0:T(8,128)S(1)}, f32[272,256]{1,0:T(8,128)S(1)}, u32[]{:S(2)}, u32[]{:S(2)}) %collective-permute-start.1) | collective-permute-done | bytes 278560 | tf_op jit(solution)/shard_map/ppermute | solution.py:264
  28.8 2.6 %collective-permute-done.6.payload = f32[272,256]{1,0:T(8,128)S(1)} collective-permute-done((f32[272,256]{1,0:T(8,128)S(1)}, f32[272,256]{1,0:T(8,128)S(1)}, u32[]{:S(2)}, u32[]{:S(2)}) %collective-permute-start.6) | collective-permute-done | bytes 278560 | tf_op jit(solution)/shard_map/ppermute | solution.py:264
  31.8 2.0 %collective-permute-start.4 = (f32[128,256]{1,0:T(8,128)S(1)}, f32[128,256]{1,0:T(8,128)S(1)}, u32[]{:S(2)}, u32[]{:S(2)}) collective-permute-start(f32[128,256]{1,0:T(8,128)S(1)} %get-tuple-element.35), channel_id=1, source_target_pairs={{0,16},{1,17},{2,18},{3,19},{4,6},{5,7},{6,4},{7,5},{8,24},{9,25},... | collective-permute-start | bytes 393224 | tf_op jit(solution)/shard_map/ppermute | solution.py:264
  33.9 1.5 %collective-permute-start.8 = (f32[128,256]{1,0:T(8,128)S(1)}, f32[128,256]{1,0:T(8,128)S(1)}, u32[]{:S(2)}, u32[]{:S(2)}) collective-permute-start(f32[128,256]{1,0:T(8,128)S(1)} %get-tuple-element.42), channel_id=1, source_target_pairs={{0,16},{1,17},{2,18},{3,19},{4,6},{5,7},{6,4},{7,5},{8,24},{9,25},... | collective-permute-start | bytes 393224 | tf_op jit(solution)/shard_map/ppermute | solution.py:264
  35.4 1.5 %collective-permute-done.4.refs_1_ = f32[128,256]{1,0:T(8,128)S(1)} collective-permute-done((f32[128,256]{1,0:T(8,128)S(1)}, f32[128,256]{1,0:T(8,128)S(1)}, u32[]{:S(2)}, u32[]{:S(2)}) %collective-permute-start.4) | collective-permute-done | bytes 131104 | tf_op jit(solution)/shard_map/ppermute | solution.py:264
  36.9 3.1 %collective-permute-start.5 = (f32[64,256]{1,0:T(8,128)S(1)}, f32[64,256]{1,0:T(8,128)S(1)}, u32[]{:S(2)}, u32[]{:S(2)}) collective-permute-start(f32[64,256]{1,0:T(8,128)S(1)} %get-tuple-element.37), channel_id=1, source_target_pairs={{0,2},{1,3},{2,0},{3,1},{4,20},{5,21},{6,22},{7,23},{8,10},{9,11},... | collective-permute-start | bytes 196616 | tf_op jit(solution)/shard_map/ppermute | solution.py:264
  40.0 1.6 %collective-permute-start.9 = (f32[64,256]{1,0:T(8,128)S(1)}, f32[64,256]{1,0:T(8,128)S(1)}, u32[]{:S(2)}, u32[]{:S(2)}) collective-permute-start(f32[64,256]{1,0:T(8,128)S(1)} %get-tuple-element.44), channel_id=1, source_target_pairs={{0,2},{1,3},{2,0},{3,1},{4,20},{5,21},{6,22},{7,23},{8,10},{9,11},... | collective-permute-start | bytes 196616 | tf_op jit(solution)/shard_map/ppermute | solution.py:264
  41.6 1.0 %collective-permute-done.5.refs_1_ = f32[64,256]{1,0:T(8,128)S(1)} collective-permute-done((f32[64,256]{1,0:T(8,128)S(1)}, f32[64,256]{1,0:T(8,128)S(1)}, u32[]{:S(2)}, u32[]{:S(2)}) %collective-permute-start.5) | collective-permute-done | bytes 65568 | tf_op jit(solution)/shard_map/ppermute | solution.py:264
  42.6 2.6 %collective-permute-done.9.refs_1_ = f32[64,256]{1,0:T(8,128)S(1)} collective-permute-done((f32[64,256]{1,0:T(8,128)S(1)}, f32[64,256]{1,0:T(8,128)S(1)}, u32[]{:S(2)}, u32[]{:S(2)}) %collective-permute-start.9) | collective-permute-done | bytes 65568 | tf_op jit(solution)/shard_map/ppermute | solution.py:264
  45.2 5.0 %collective-permute-start.14 = (f32[64,256]{1,0:T(8,128)S(1)}, f32[64,256]{1,0:T(8,128)S(1)}, u32[]{:S(2)}, u32[]{:S(2)}) collective-permute-start(f32[64,256]{1,0:T(8,128)S(1)} %intensity.1.refs_0_), channel_id=1, source_target_pairs={{0,27},{1,26},{2,25},{3,24},{4,31},{5,30},{6,29},{7,28},{8,19},{9,... | collective-permute-start | bytes 196616 | tf_op jit(solution)/shard_map/ppermute | solution.py:264
  50.2 0.6 collective-permute-start.13
  50.8 0.7 %collective-permute-start.10 = (f32[64,256]{1,0:T(8,128)S(1)}, f32[64,256]{1,0:T(8,128)S(1)}, u32[]{:S(2)}, u32[]{:S(2)}) collective-permute-start(f32[64,256]{1,0:T(8,128)S(1)} %intensity.1.refs_0_), channel_id=1, source_target_pairs={{0,3},{1,2},{2,1},{3,0},{4,7},{5,6},{6,5},{7,4},{8,11},{9,10},{10,... | collective-permute-start | bytes 196616 | tf_op jit(solution)/shard_map/ppermute | solution.py:264
  51.5 1.8 %collective-permute-done.14.refs_5_ = f32[64,256]{1,0:T(8,128)S(1)} collective-permute-done((f32[64,256]{1,0:T(8,128)S(1)}, f32[64,256]{1,0:T(8,128)S(1)}, u32[]{:S(2)}, u32[]{:S(2)}) %collective-permute-start.14) | collective-permute-done | bytes 65568 | tf_op jit(solution)/shard_map/ppermute | solution.py:264
  53.3 2.1 %collective-permute-done.13.refs_4_ = f32[64,256]{1,0:T(8,128)S(1)} collective-permute-done((f32[64,256]{1,0:T(8,128)S(1)}, f32[64,256]{1,0:T(8,128)S(1)}, u32[]{:S(2)}, u32[]{:S(2)}) %collective-permute-start.13) | collective-permute-done | bytes 65568 | tf_op jit(solution)/shard_map/ppermute | solution.py:264
  55.4 1.5 %collective-permute-done.10.refs_1_ = f32[64,256]{1,0:T(8,128)S(1)} collective-permute-done((f32[64,256]{1,0:T(8,128)S(1)}, f32[64,256]{1,0:T(8,128)S(1)}, u32[]{:S(2)}, u32[]{:S(2)}) %collective-permute-start.10) | collective-permute-done | bytes 65568 | tf_op jit(solution)/shard_map/ppermute | solution.py:264
  56.9 1.2 %collective-permute-done.12.refs_3_ = f32[64,256]{1,0:T(8,128)S(1)} collective-permute-done((f32[64,256]{1,0:T(8,128)S(1)}, f32[64,256]{1,0:T(8,128)S(1)}, u32[]{:S(2)}, u32[]{:S(2)}) %collective-permute-start.12) | collective-permute-done | bytes 65568 | tf_op jit(solution)/shard_map/ppermute | solution.py:264
  58.1 1.0 %unfold.1 = f32[512,256]{1,0:T(8,128)} custom-call(f32[64,256]{1,0:T(8,128)S(1)} %intensity.1.refs_0_, f32[64,256]{1,0:T(8,128)S(1)} %collective-permute-done.10.refs_1_, f32[64,256]{1,0:T(8,128)S(1)} %collective-permute-done.11.refs_2_, f32[64,256]{1,0:T(8,128)S(1)} %collective-permute-done.12.refs_3_, f32[64,256]{1,0:T(8,128)S(1)} %collective-permute-done.13.refs_4_, ...), custom_call_target="tpu_custom_call" | custom-call | flops 1 | bytes 1 | tf_op jit(solution)/shard_map/unfold/pallas_call | solution.py:251
  (29 shorter events, 1.7 us)
Async XLA Ops:
  15.4 6.2 %collective-permute-start = (f32[136,256]{1,0:T(8,128)}, f32[136,256]{1,0:T(8,128)S(1)}, u32[]{:S(2)}, u32[]{:S(2)}) collective-permute-start(f32[136,256]{1,0:T(8,128)} %get-tuple-element.25.first), channel_id=1, source_target_pairs={{0,8},{1,9},{2,10},{3,11},{4,5},{5,4},{6,7},{7,6},{8,0},{9,1},{10,... | collective-permute-start | bytes 417800 | tf_op jit(solution)/shard_map/ppermute | solution.py:264
  18.4 5.5 %collective-permute-start.2 = (f32[136,256]{1,0:T(8,128)}, f32[136,256]{1,0:T(8,128)S(1)}, u32[]{:S(2)}, u32[]{:S(2)}) collective-permute-start(f32[136,256]{1,0:T(8,128)} %get-tuple-element.26.second), channel_id=1, source_target_pairs={{0,8},{1,9},{2,10},{3,11},{4,5},{5,4},{6,7},{7,6},{8,0},{9,1},{10,... | collective-permute-start | bytes 417800 | tf_op jit(solution)/shard_map/ppermute | solution.py:264
  18.5 0.9 %copy-start = (f32[136,256]{1,0:T(8,128)S(1)}, f32[136,256]{1,0:T(8,128)}, u32[]{:S(2)}) copy-start(f32[136,256]{1,0:T(8,128)} %get-tuple-element.26.second) | copy-start | bytes 417796
  19.4 0.9 %copy-start.1 = (f32[136,256]{1,0:T(8,128)S(1)}, f32[136,256]{1,0:T(8,128)}, u32[]{:S(2)}) copy-start(f32[136,256]{1,0:T(8,128)} %get-tuple-element.25.first) | copy-start | bytes 417796
  21.6 6.7 %collective-permute-start.1 = (f32[272,256]{1,0:T(8,128)S(1)}, f32[272,256]{1,0:T(8,128)S(1)}, u32[]{:S(2)}, u32[]{:S(2)}) collective-permute-start(f32[272,256]{1,0:T(8,128)S(1)} %join.2.payload.rest_0_), channel_id=1, source_target_pairs={{0,1},{1,0},{2,3},{3,2},{4,12},{5,13},{6,14},{7,15},{8,9},{9,8},{1... | collective-permute-start | bytes 835592 | tf_op jit(solution)/shard_map/ppermute | solution.py:264
  23.9 7.5 %collective-permute-start.6 = (f32[272,256]{1,0:T(8,128)S(1)}, f32[272,256]{1,0:T(8,128)S(1)}, u32[]{:S(2)}, u32[]{:S(2)}) collective-permute-start(f32[272,256]{1,0:T(8,128)S(1)} %join.3.payload), channel_id=1, source_target_pairs={{0,1},{1,0},{2,3},{3,2},{4,12},{5,13},{6,14},{7,15},{8,9},{9,8},{1... | collective-permute-start | bytes 835592 | tf_op jit(solution)/shard_map/ppermute | solution.py:264
  28.7 3.1 %collective-permute-start.3 = (f32[256,256]{1,0:T(8,128)S(1)}, f32[256,256]{1,0:T(8,128)S(1)}, u32[]{:S(2)}, u32[]{:S(2)}) collective-permute-start(f32[256,256]{1,0:T(8,128)S(1)} %get-tuple-element.33), channel_id=1, source_target_pairs={{0,4},{1,5},{2,6},{3,7},{4,0},{5,1},{6,2},{7,3},{8,12},{9,13},{10,... | collective-permute-start | bytes 786440 | tf_op jit(solution)/shard_map/ppermute | solution.py:264
  31.7 2.2 %collective-permute-start.7 = (f32[256,256]{1,0:T(8,128)S(1)}, f32[256,256]{1,0:T(8,128)S(1)}, u32[]{:S(2)}, u32[]{:S(2)}) collective-permute-start(f32[256,256]{1,0:T(8,128)S(1)} %get-tuple-element.40), channel_id=1, source_target_pairs={{0,4},{1,5},{2,6},{3,7},{4,0},{5,1},{6,2},{7,3},{8,12},{9,13},{10,... | collective-permute-start | bytes 786440 | tf_op jit(solution)/shard_map/ppermute | solution.py:264
  31.8 5.0 %collective-permute-start.4 = (f32[128,256]{1,0:T(8,128)S(1)}, f32[128,256]{1,0:T(8,128)S(1)}, u32[]{:S(2)}, u32[]{:S(2)}) collective-permute-start(f32[128,256]{1,0:T(8,128)S(1)} %get-tuple-element.35), channel_id=1, source_target_pairs={{0,16},{1,17},{2,18},{3,19},{4,6},{5,7},{6,4},{7,5},{8,24},{9,25},... | collective-permute-start | bytes 393224 | tf_op jit(solution)/shard_map/ppermute | solution.py:264
  33.9 6.1 %collective-permute-start.8 = (f32[128,256]{1,0:T(8,128)S(1)}, f32[128,256]{1,0:T(8,128)S(1)}, u32[]{:S(2)}, u32[]{:S(2)}) collective-permute-start(f32[128,256]{1,0:T(8,128)S(1)} %get-tuple-element.42), channel_id=1, source_target_pairs={{0,16},{1,17},{2,18},{3,19},{4,6},{5,7},{6,4},{7,5},{8,24},{9,25},... | collective-permute-start | bytes 393224 | tf_op jit(solution)/shard_map/ppermute | solution.py:264
  36.9 5.7 %collective-permute-start.5 = (f32[64,256]{1,0:T(8,128)S(1)}, f32[64,256]{1,0:T(8,128)S(1)}, u32[]{:S(2)}, u32[]{:S(2)}) collective-permute-start(f32[64,256]{1,0:T(8,128)S(1)} %get-tuple-element.37), channel_id=1, source_target_pairs={{0,2},{1,3},{2,0},{3,1},{4,20},{5,21},{6,22},{7,23},{8,10},{9,11},... | collective-permute-start | bytes 196616 | tf_op jit(solution)/shard_map/ppermute | solution.py:264
  40.0 5.2 %collective-permute-start.9 = (f32[64,256]{1,0:T(8,128)S(1)}, f32[64,256]{1,0:T(8,128)S(1)}, u32[]{:S(2)}, u32[]{:S(2)}) collective-permute-start(f32[64,256]{1,0:T(8,128)S(1)} %get-tuple-element.44), channel_id=1, source_target_pairs={{0,2},{1,3},{2,0},{3,1},{4,20},{5,21},{6,22},{7,23},{8,10},{9,11},... | collective-permute-start | bytes 196616 | tf_op jit(solution)/shard_map/ppermute | solution.py:264
  45.2 8.0 %collective-permute-start.14 = (f32[64,256]{1,0:T(8,128)S(1)}, f32[64,256]{1,0:T(8,128)S(1)}, u32[]{:S(2)}, u32[]{:S(2)}) collective-permute-start(f32[64,256]{1,0:T(8,128)S(1)} %intensity.1.refs_0_), channel_id=1, source_target_pairs={{0,27},{1,26},{2,25},{3,24},{4,31},{5,30},{6,29},{7,28},{8,19},{9,... | collective-permute-start | bytes 196616 | tf_op jit(solution)/shard_map/ppermute | solution.py:264
  50.2 5.2 %collective-permute-start.13 = (f32[64,256]{1,0:T(8,128)S(1)}, f32[64,256]{1,0:T(8,128)S(1)}, u32[]{:S(2)}, u32[]{:S(2)}) collective-permute-start(f32[64,256]{1,0:T(8,128)S(1)} %intensity.1.refs_0_), channel_id=1, source_target_pairs={{0,24},{1,25},{2,26},{3,27},{4,28},{5,29},{6,30},{7,31},{8,16},{9,... | collective-permute-start | bytes 196616 | tf_op jit(solution)/shard_map/ppermute | solution.py:264
  50.8 6.1 %collective-permute-start.10 = (f32[64,256]{1,0:T(8,128)S(1)}, f32[64,256]{1,0:T(8,128)S(1)}, u32[]{:S(2)}, u32[]{:S(2)}) collective-permute-start(f32[64,256]{1,0:T(8,128)S(1)} %intensity.1.refs_0_), channel_id=1, source_target_pairs={{0,3},{1,2},{2,1},{3,0},{4,7},{5,6},{6,5},{7,4},{8,11},{9,10},{10,... | collective-permute-start | bytes 196616 | tf_op jit(solution)/shard_map/ppermute | solution.py:264
  51.5 5.4 %collective-permute-start.11 = (f32[64,256]{1,0:T(8,128)S(1)}, f32[64,256]{1,0:T(8,128)S(1)}, u32[]{:S(2)}, u32[]{:S(2)}) collective-permute-start(f32[64,256]{1,0:T(8,128)S(1)} %intensity.1.refs_0_), channel_id=1, source_target_pairs={{0,4},{1,5},{2,6},{3,7},{4,0},{5,1},{6,2},{7,3},{8,12},{9,13},{10,... | collective-permute-start | bytes 196616 | tf_op jit(solution)/shard_map/ppermute | solution.py:264
  53.3 3.6 %collective-permute-start.16 = (f32[64,256]{1,0:T(8,128)S(1)}, f32[64,256]{1,0:T(8,128)S(1)}, u32[]{:S(2)}, u32[]{:S(2)}) collective-permute-start(f32[64,256]{1,0:T(8,128)S(1)} %collective-permute-done.14.refs_5_), channel_id=1, source_target_pairs={{0,4},{1,5},{2,6},{3,7},{4,0},{5,1},{6,2},{7,3},{8,12},{9,13},{10,... | collective-permute-start | bytes 196616 | tf_op jit(solution)/shard_map/ppermute | solution.py:264
  55.4 1.5 %collective-permute-start.15 = (f32[64,256]{1,0:T(8,128)S(1)}, f32[64,256]{1,0:T(8,128)S(1)}, u32[]{:S(2)}, u32[]{:S(2)}) collective-permute-start(f32[64,256]{1,0:T(8,128)S(1)} %collective-permute-done.13.refs_4_), channel_id=1, source_target_pairs={{0,4},{1,5},{2,6},{3,7},{4,0},{5,1},{6,2},{7,3},{8,12},{9,13},{10,... | collective-permute-start | bytes 196616 | tf_op jit(solution)/shard_map/ppermute | solution.py:264
  56.9 1.3 %collective-permute-start.12 = (f32[64,256]{1,0:T(8,128)S(1)}, f32[64,256]{1,0:T(8,128)S(1)}, u32[]{:S(2)}, u32[]{:S(2)}) collective-permute-start(f32[64,256]{1,0:T(8,128)S(1)} %collective-permute-done.10.refs_1_), channel_id=1, source_target_pairs={{0,4},{1,5},{2,6},{3,7},{4,0},{5,1},{6,2},{7,3},{8,12},{9,13},{10,... | collective-permute-start | bytes 196616 | tf_op jit(solution)/shard_map/ppermute | solution.py:264
